TPU v7x, 128 devices: a whole 4x4x4 slice. The times are simulated.
128 devices in a mesh: dap: 32 (over y_lo, x, z), grp: 4 (over y_hi, core).
Axes of the slice: x: 4, y: 4 (y_hi: 2, y_lo: 2; y = y_hi * 2 + y_lo), z: 4, core: 2. Of those that a mesh axis runs over, the one named last changes fastest.
Arguments:
- homolog_stack: float32 [128, 512, 256], P('dap'), may hold values from -6 to 6
- couple_score_offset: float32 [8, 512, 512], P('grp', 'dap'), may hold values from -250 to 250
- strand_identity: int32 [512], replicated, may hold values from 0 to 3, never falling along the last dimension, each value on 1 to 256 neighbouring positions
- strand_score_offset: float32 [8], P('grp'), may hold values from -2 to 2
- homolog_presence: int32 [128], replicated, may hold values from 0 to 1, as said below
- horizontal_matrix: float32 [4, 256, 256], P(None, None, 'grp'), may hold values from -0.375 to 0.375
- horizontal_final_matrix: float32 [256, 256], P('grp'), may hold values from -0.375 to 0.375
- vertical_matrix: float32 [4, 256, 256], replicated, may hold values from -4 to 4
- vertical_final_matrix: float32 [256, 256], replicated, may hold values from -0.375 to 0.375
- expand_matrix: float32 [256, 1024], replicated, may hold values from -0.375 to 0.375
- shrink_matrix: float32 [1024, 256], replicated, may hold values from -0.1875 to 0.1875
- tensor_matrix: float32 [2, 256, 32], replicated, may hold values from -0.375 to 0.375
- couple_matrix: float32 [1024, 128], replicated, may hold values from -1 to 1
Outputs:
- revised_homolog_stack: float32 [128, 512, 256], P(None, ('dap', 'grp'))
- pair_outer_update: float32 [512, 512, 128], P('dap', 'grp')
Inputs may be any that keep to these rules, and one draw needn't show every extreme that they name: `homolog_presence`: row 0 is always live.
All inputs are finite; a program needn't handle non-finite values.
Results may differ from a plain program's by a relative error of at most 0.0003.
Values sent between devices are 32-bit elements; how exact they have to be, the bound alone decides.
A program may use at most 192 MiB of HBM per device.

v0:
```python
import jax
import jax.numpy as jnp
from jax import lax
from jax.sharding import PartitionSpec as P

FOCUS_GROUPS = 8
GROUP_BREADTH = 32
TENSOR_BREADTH = 32
PAIR_DIM = 128


HIGH_PRECISION = lax.Precision.HIGHEST


def standardize_entries(value_rows):
    center = value_rows - jnp.mean(value_rows, axis=-1, keepdims=True)
    spread = jnp.mean(center * center, axis=-1, keepdims=True)
    return center * lax.rsqrt(spread + 1e-05)


def outer_project(left_factor, right, couple_matrix):
    outer = jnp.einsum("sic,sje->ijce", left_factor, right, precision=HIGH_PRECISION)
    count_left, count_right = (outer.shape[0], outer.shape[1])
    flat = outer.reshape(count_left * count_right, TENSOR_BREADTH * TENSOR_BREADTH)
    return jnp.dot(flat, couple_matrix, precision=HIGH_PRECISION).reshape(
        count_left, count_right, PAIR_DIM
    )


def body(
    homolog_stack,
    couple_score_offset,
    strand_identity,
    strand_score_offset,
    homolog_presence,
    horizontal_matrix,
    horizontal_final_matrix,
    vertical_matrix,
    vertical_final_matrix,
    expand_matrix,
    shrink_matrix,
    tensor_matrix,
    couple_matrix,
):
    parallel_degree = lax.axis_size("dap")
    grp_size = lax.axis_size("grp")
    grp_index = lax.axis_index("grp")
    shard_homologs, amino_total, embedding_breadth = homolog_stack.shape
    local_residue_count = amino_total // parallel_degree
    quarter = local_residue_count // grp_size
    heads_here = horizontal_matrix.shape[2] // GROUP_BREADTH
    scale = 1.0 / jnp.sqrt(jnp.float32(GROUP_BREADTH))
    same = (strand_identity[:, None] == strand_identity[None, :]).astype(jnp.float32)
    standardized_source = standardize_entries(homolog_stack)
    projected = jnp.einsum(
        "src,kce->ksre", standardized_source, horizontal_matrix, precision=HIGH_PRECISION
    )
    projected = projected.reshape(4, shard_homologs, amino_total, heads_here, GROUP_BREADTH)
    queries, keyed, valued, gating = (projected[0], projected[1], projected[2], projected[3])
    piece = lax.all_gather(couple_score_offset, "dap", axis=1, tiled=True)
    count = piece.shape[1]
    biased = piece + strand_score_offset[:, None, None] * same[None]

    def one_row(parts):
        query, key_row, value_row, gate = parts
        gate_rows = gate.reshape(count, heads_here * GROUP_BREADTH)
        logits = jnp.einsum("ihd,jhd->hij", query, key_row, precision=HIGH_PRECISION) * scale
        weights = jax.nn.softmax(logits + biased, axis=-1)
        attended_rows = jnp.einsum(
            "hij,jhd->ihd", weights, value_row, precision=HIGH_PRECISION
        ).reshape(count, heads_here * GROUP_BREADTH)
        attended_rows = attended_rows * jax.nn.sigmoid(gate_rows)
        return jnp.dot(attended_rows, horizontal_final_matrix, precision=HIGH_PRECISION)

    partial_rows = lax.map(one_row, (queries, keyed, valued, gating))
    live_rows = homolog_presence.astype(jnp.float32)
    mask_bias = (live_rows - 1.0) * 1000000000.0
    live = jnp.sum(live_rows)
    accumulated_tensor = lax.psum(partial_rows, "grp")
    revised_tensor = (homolog_stack + accumulated_tensor).reshape(
        shard_homologs, parallel_degree, local_residue_count, embedding_breadth
    )
    moved = lax.all_to_all(revised_tensor, "dap", split_axis=1, concat_axis=0, tiled=True)
    mine = lax.dynamic_slice_in_dim(moved, grp_index * quarter, quarter, 2)
    rows = mine.shape[0]
    column_count = mine.shape[2]
    current_block = mine.reshape(rows, column_count, embedding_breadth)
    col_normed = standardize_entries(current_block)
    col_proj = jnp.einsum("snc,kce->ksne", col_normed, vertical_matrix, precision=HIGH_PRECISION)
    col_proj = col_proj.reshape(4, rows, column_count, FOCUS_GROUPS, GROUP_BREADTH)
    logits = (
        jnp.einsum("snhd,tnhd->nhst", col_proj[0], col_proj[1], precision=HIGH_PRECISION) * scale
    )
    logits = logits + mask_bias[None, None, None, :]
    weights = jax.nn.softmax(logits, axis=-1)
    attended_rows = jnp.einsum("nhst,tnhd->snhd", weights, col_proj[2], precision=HIGH_PRECISION)
    attended_rows = attended_rows.reshape(
        rows, column_count, FOCUS_GROUPS * GROUP_BREADTH
    ) * jax.nn.sigmoid(col_proj[3].reshape(rows, column_count, FOCUS_GROUPS * GROUP_BREADTH))
    first_factor = current_block + jnp.einsum(
        "owq,qg->owg", attended_rows, vertical_final_matrix, precision=HIGH_PRECISION
    )
    hidden_units = jax.nn.relu(
        jnp.einsum(
            "dgz,zb->dgb",
            standardize_entries(first_factor),
            expand_matrix,
            precision=HIGH_PRECISION,
        )
    )
    right_operand = first_factor + jnp.einsum(
        "owq,qg->owg", hidden_units, shrink_matrix, precision=HIGH_PRECISION
    )
    outer_in = jnp.einsum(
        "snc,kce->ksne", standardize_entries(right_operand), tensor_matrix, precision=HIGH_PRECISION
    )
    outer_in = outer_in * live_rows[None, :, None, None]
    joined_parts = jnp.concatenate([outer_in[0], outer_in[1]], axis=-1)
    gathered = lax.all_gather(joined_parts, "grp", axis=1, tiled=True)
    left_factor = gathered[:, :, :TENSOR_BREADTH]
    row_part = gathered.shape[0] // grp_size
    right_rows = lax.dynamic_slice_in_dim(
        gathered[:, :, TENSOR_BREADTH:], grp_index * row_part, row_part, 0
    )
    right_wide = lax.all_gather(right_rows, "dap", axis=1, tiled=True)
    right = lax.all_to_all(right_wide, "grp", split_axis=1, concat_axis=0, tiled=True)
    pair_outer_update = outer_project(left_factor, right, couple_matrix) / live
    return (right_operand, pair_outer_update)


def solution(mesh):
    return jax.shard_map(
        body,
        mesh=mesh,
        in_specs=(
            P("dap", None, None),
            P("grp", "dap", None),
            P(),
            P("grp"),
            P(),
            P(None, None, "grp"),
            P("grp", None),
            P(),
            P(),
            P(),
            P(),
            P(),
            P(),
        ),
        out_specs=(P(None, ("dap", "grp"), None), P("dap", "grp", None)),
        check_vma=False,
    )
```

profile of v0, /device:TPU:1, one launch (start us, length us, event | category | flops | bytes accessed | tf_op | source)
XLA Modules:
  0.0 602.8 jit_solution(10975055227117202461)
XLA Ops:
  12.8 2.6 fusion.23
  16.8 128.8 %all-gather.3.cloned.1.call-done = f32[2,512,512]{2,0,1:T(2,128)} async-done(((f32[2,16,512]{2,0,1:T(2,128)}), f32[2,512,512]{2,0,1:T(2,128)}) %all-gather.3.cloned.1.call-update) | async-done | bytes 2097168 | tf_op jit(solution)/shard_map/all_gather | solution.py:60
  145.5 4.1 multiply_add_fusion.2
  149.6 2.8 copy.56
  152.4 32.3 %while.10 = (s32[]{:T(128)}, f32[4,512,256]{2,1,0:T(8,128)}, f32[4,512,2,32]{1,3,2,0:T(8,128)}, f32[4,512,2,32]{1,3,2,0:T(8,128)}, f32[4,512,2,32]{1,3,2,0:T(8,1...) while((s32[]{:T(128)}, f32[4,512,256]{2,1,0:T(8,128)}, ...), condition=%wide.region_5.6_spmd, body=%wide.region_2.5_spmd.sunk | while | flops 507115520 | bytes 10310769 | solution.py:75
  153.4 2.9 fusion.96
  156.6 2.5 fusion.98
  161.4 2.9 fusion.96
  164.6 2.5 fusion.98
  169.5 2.9 fusion.96
  172.7 2.5 fusion.98
  177.6 2.9 fusion.96
  180.8 2.5 fusion.98
  184.7 80.1 %all-reduce.2.cloned.1.call-done = f32[4,512,256]{2,1,0:T(8,128)} async-done(((f32[4,512,256]{2,1,0:T(8,128)}), f32[4,512,256]{2,1,0:T(8,128)}) %all-reduce.2.cloned.1.call-update) | async-done | bytes 2097168 | tf_op jit(solution)/shard_map/psum | solution.py:79
  268.3 7.1 %all-to-all-start = ((f32[4,32,16,256]{3,2,0,1:T(8,128)}), f32[4,32,16,256]{3,2,0,1:T(8,128)S(1)}, u32[]{:S(2)}, u32[]{:S(2)}) async-start(f32[4,32,16,256]{3,2,0,1:T(8,128)} %copy.57), calls=%async_computation | async-start | bytes 4194304 | tf_op jit(solution)/shard_map/all_to_all | solution.py:83
  276.3 26.9 %all-to-all-done = f32[4,32,16,256]{3,2,0,1:T(8,128)S(1)} async-done(((f32[4,32,16,256]{3,2,0,1:T(8,128)}), f32[4,32,16,256]{3,2,0,1:T(8,128)S(1)}, u32[]{:S(2)}, u32[]{:S(2)}) %all-to-all-start) | async-done | bytes 2097184 | tf_op jit(solution)/shard_map/all_to_all | solution.py:83
  306.9 3.0 convolution_bitcast_fusion.2
  312.4 2.0 copy.59
  314.5 3.5 fusion.22
  318.5 2.3 fusion.19
  325.9 2.4 fusion.76
  329.3 9.9 %all_gather.10 = f32[128,16,64]{0,2,1:T(8,128)S(1)} all-gather(f32[128,4,64]{0,2,1:T(8,128)S(1)} %pad_maximum_fusion), channel_id=1, replica_groups=mesh['dap'=32,'grp'=4] {'grp'}, dimensions={1}, use_global_device_ids=true | all-gather | bytes 655360 | tf_op jit(solution)/shard_map/all_gather | solution.py:119
  340.2 147.0 %all-gather.5.cloned.1.call-done = f32[32,512,32]{2,0,1:T(8,128)} async-done(((f32[32,16,32]{2,0,1:T(8,128)}), f32[32,512,32]{2,0,1:T(8,128)}) %all-gather.5.cloned.1.call-update) | async-done | bytes 2097168 | tf_op jit(solution)/shard_map/all_gather | solution.py:125
  487.2 7.1 %reshape.150 = f32[4,1,131072]{2,1,0:T(1,128)} reshape(f32[512,32,32]{2,1,0:T(8,128)} %bitcast.152) | data formatting | bytes 4194304
  494.3 22.8 %all-to-all-start.1 = ((f32[4,1,131072]{2,1,0:T(1,128)}), f32[4,1,131072]{2,1,0:T(1,128)S(1)}, u32[]{:S(2)}, u32[]{:S(2)}) async-start(f32[4,1,131072]{2,1,0:T(1,128)} %reshape.150), calls=%async_computation.1 | async-start | bytes 4194304 | tf_op jit(solution)/shard_map/all_to_all | solution.py:126
  518.3 25.2 %all-to-all-done.1 = f32[4,1,131072]{2,1,0:T(1,128)S(1)} async-done(((f32[4,1,131072]{2,1,0:T(1,128)}), f32[4,1,131072]{2,1,0:T(1,128)S(1)}, u32[]{:S(2)}, u32[]{:S(2)}) %all-to-all-start.1) | async-done | bytes 2097184 | tf_op jit(solution)/shard_map/all_to_all | solution.py:126
  545.3 7.7 %reduce.1 = f32[4,131072]{1,0:T(4,128)S(1)} reduce(f32[4,1,131072]{2,1,0:T(1,128)} %copy-done.4, f32[]{:T(128)} %broadcast.150), dimensions={1}, to_apply=%all_to_all.30.reduce_sub_computation | reduce | bytes 4194308 | tf_op jit(solution)/shard_map/all_to_all | solution.py:126
  553.0 6.1 %reshape.151 = f32[512,32,32]{2,1,0:T(8,128)} reshape(f32[4,131072]{1,0:T(4,128)S(1)} %reduce.1) | data formatting | bytes 4194304
  559.2 7.2 %copy.66 = f32[32,4,128,32]{2,0,1,3:T(8,128)S(1)} copy(f32[32,4,128,32]{3,0,2,1:T(8,128)} %bitcast.150) | data formatting | bytes 4194304 | tf_op jit(solution)/shard_map/all_to_all | solution.py:126
  566.4 7.0 %convolution_bitcast_fusion.1 = f32[16,128,32,32]{1,2,0,3:T(8,128)S(1)} fusion(f32[128,128,32,1]{1,0,3,2:T(8,128)S(1)} %bitcast.154, f32[128,16,64]{0,2,1:T(8,128)S(1)} %all_gather.10), kind=kOutput, calls=%fused_computation.19 | convolution fusion | flops 3221225472 | bytes 10747904 | tf_op jit(solution)/shard_map/sic,sje->ijce/dot_general | solution.py:22
  573.5 6.7 %copy.67 = f32[16,128,32,32]{1,3,2,0:T(8,128)S(1)} copy(f32[16,128,32,32]{1,2,0,3:T(8,128)S(1)} %convolution_bitcast_fusion.1) | data formatting | bytes 16777216 | tf_op jit(solution)/shard_map/sic,sje->ijce/transpose | solution.py:22
  580.2 15.7 %convolution_divide_fusion = f32[16,128,128]{2,1,0:T(8,128)} fusion(f32[16,128,1024]{1,2,0:T(8,128)S(1)} %bitcast.151, f32[1024,128]{1,0:T(8,128)S(1)} %copy-done.12, f32[]{:T(128)} %get-tuple-element.98), kind=kOutput, calls=%fused_computation.36 | convolution fusion | flops 3221487616 | bytes 9961476 | tf_op jit(solution)/shard_map/dot_general | solution.py:25
  (100 shorter events, 38.8 us)
Async XLA Ops:
  7.2 299.7 %copy-start = (f32[4,256,256]{2,1,0:T(8,128)S(1)}, f32[4,256,256]{2,1,0:T(8,128)}, u32[]{:S(2)}) copy-start(f32[4,256,256]{2,1,0:T(8,128)} %param.22) | copy-start | bytes 3145732
  7.2 3.8 copy-start.2
  7.2 138.3 %all-gather.3.cloned.1.call-start = ((), (), s32[]{:S(2)}) async-start(), calls=%async_computation.2 | async-start | bytes 2162688 | tf_op jit(solution)/shard_map/all_gather | solution.py:60
  8.9 255.9 %all-reduce.2.cloned.1.call-start = ((), (), s32[]{:S(2)}) async-start(), calls=%async_computation.3 | async-start | bytes 4194304 | tf_op jit(solution)/shard_map/psum | solution.py:79
  9.0 2.7 copy-start.16
  11.0 1.8 copy-start.14
  15.4 130.1 %copy-start.7 = (f32[512,512]{1,0:T(8,128)S(1)}, f32[512,512]{1,0:T(8,128)}, u32[]{:S(2)}) copy-start(f32[512,512]{1,0:T(8,128)} %compare_convert_fusion) | copy-start | bytes 3145732
  15.4 130.1 %copy-start.17 = (f32[2]{0:T(128)S(1)}, f32[2]{0:T(128)}, u32[]{:S(2)}) copy-start(f32[2]{0:T(128)} %param.18) | copy-start | bytes 28
  149.6 2.8 copy-start.9
  184.7 80.1 %copy-start.3 = (f32[4,512,256]{2,1,0:T(8,128)S(1)}, f32[4,512,256]{2,1,0:T(8,128)}, u32[]{:S(2)}) copy-start(f32[4,512,256]{2,1,0:T(8,128)} %param.15) | copy-start | bytes 6291460
  268.3 7.4 %copy-start.19 = (s32[128]{0:T(128)S(1)}, s32[128]{0:T(128)}, u32[]{:S(2)}) copy-start(s32[128]{0:T(128)} %param.19) | copy-start | bytes 1540
  268.3 35.0 %all-to-all-start = ((f32[4,32,16,256]{3,2,0,1:T(8,128)}), f32[4,32,16,256]{3,2,0,1:T(8,128)S(1)}, u32[]{:S(2)}, u32[]{:S(2)}) async-start(f32[4,32,16,256]{3,2,0,1:T(8,128)} %copy.57), calls=%async_computation | async-start | bytes 4194304 | tf_op jit(solution)/shard_map/all_to_all | solution.py:83
  275.4 211.8 %all-gather.5.cloned.1.call-start = ((), (), s32[]{:S(2)}) async-start(), calls=%async_computation.4 | async-start | bytes 8650752 | tf_op jit(solution)/shard_map/all_gather | solution.py:125
  303.3 1.4 copy-start.8
  306.1 0.8 copy-start.5
  314.5 4.0 copy-start.13
  318.5 3.3 copy-start.6
  318.5 3.3 copy-start.18
  321.8 2.1 copy-start.10
  323.7 2.2 copy-start.11
  325.9 2.7 copy-start.15
  494.3 49.2 %all-to-all-start.1 = ((f32[4,1,131072]{2,1,0:T(1,128)}), f32[4,1,131072]{2,1,0:T(1,128)S(1)}, u32[]{:S(2)}, u32[]{:S(2)}) async-start(f32[4,1,131072]{2,1,0:T(1,128)} %reshape.150), calls=%async_computation.1 | async-start | bytes 4194304 | tf_op jit(solution)/shard_map/all_to_all | solution.py:126
  543.5 1.4 copy-start.4
  573.4 6.7 %copy-start.12 = (f32[1024,128]{1,0:T(8,128)S(1)}, f32[1024,128]{1,0:T(8,128)}, u32[]{:S(2)}) copy-start(f32[1024,128]{1,0:T(8,128)} %param.27) | copy-start | bytes 1572868
  580.2 15.7 %copy-start.1 = (f32[4,256,256]{2,1,0:T(8,128)S(1)}, f32[4,256,256]{2,1,0:T(8,128)}, u32[]{:S(2)}) copy-start(f32[4,256,256]{2,1,0:T(8,128)} %param.22) | copy-start | bytes 3145732
Sparse Core Ops, SparseCore 0:
  9.7 135.8 all-gather.2
  184.8 79.9 all-reduce.1
  340.4 146.7 all-gather.4
where the time goes:
time: 611 us; the launch traced here: 603 us
  waiting for transfers between devices  408 us (67%)
  matrix products  68.1 us (11%)
  local copies, waits for them, and re-layouts  46 us (8%)
  starting transfers between devices  30.3 us (5%)
  other arithmetic  25.9 us (4%)
  between operations  14.5 us (2%)
  blocking collectives  9.9 us (2%)
    all_gather x1, waiting for transfers between devices, body(): right_wide = lax.all_gather(right_rows, 'dap', axis=1, tiled=True)  147 us
    all_gather x1, waiting for transfers between devices, body(): piece = lax.all_gather(couple_score_offset, 'dap', axis=1, tiled=True)  129 us
    psum x1, waiting for transfers between devices, body(): accumulated_tensor = lax.psum(partial_rows, 'grp')  80.1 us
    all_to_all x1, waiting for transfers between devices, body(): lax.all_to_all(revised_tensor, 'dap', split_axis=1, concat_axis=0, tiled=...  26.9 us
    all_to_all x1, waiting for transfers between devices, body(): lax.all_to_all(right_wide, 'grp', split_axis=1, concat_axis=0, tiled=True)  25.2 us
    all_to_all x1, starting transfers between devices, body(): lax.all_to_all(right_wide, 'grp', split_axis=1, concat_axis=0, tiled=True)  22.8 us
    unnamed x45, local copies, waits for them, and re-layouts  19.3 us
    dot_general x1, matrix products, outer_project(): jnp.dot(flat, couple_matrix, precision=HIGH_PRECISION)  15.7 us
  transfers between devices with their start and end apart: 5, of which 5 were waited for; matrix products, arithmetic and copies ran while one was open for 2% of the time, Pallas kernels for 0%

commit v1 on v0

v1 whole, which is shorter than its diff:
```python
import functools
import math

import jax
import jax.numpy as jnp
from jax import lax
from jax.experimental import pallas as pl
from jax.experimental.pallas import tpu as pltpu
from jax.sharding import PartitionSpec as P

F32 = jnp.float32
BF16 = jnp.bfloat16
MESH = pl.DeviceIdType.MESH
HEAD = 32
LOG2E = math.log2(math.e)
NN = (((1,), (0,)), ((), ()))
NT = (((1,), (1,)), ((), ()))


def split(a):
    high = a.astype(BF16)
    return high, (a - high.astype(F32)).astype(BF16)


def dot(a, b, dims=NN):
    return lax.dot_general(a, b, dims, preferred_element_type=F32)


def dot3(a, b, dims=NN):
    return dot(a[0], b[0], dims) + (dot(a[0], b[1], dims) + dot(a[1], b[0], dims))


def normed(rows):
    center = rows - jnp.mean(rows, axis=-1, keepdims=True)
    spread = jnp.mean(center * center, axis=-1, keepdims=True)
    return center * lax.rsqrt(spread + 1e-05)


def merge_halves(a, b):
    upper = lax.broadcasted_iota(jnp.int32, a.shape, a.ndim - 2) < 4
    first = jnp.where(upper, a, pltpu.roll(b, 4, axis=b.ndim - 2))
    second = jnp.where(upper, pltpu.roll(a, 4, axis=a.ndim - 2), b)
    return first, second


def lane_iota(shape):
    return lax.broadcasted_iota(jnp.int32, shape, len(shape) - 1)


def drain(ref, sem):
    pltpu.make_async_copy(ref, ref, sem).wait()


def row_kernel(
    x_ref, bias_ref, ids_ref, offset_ref, weight_ref, final_ref,
    xr_ref, or_ref, finals_ref,
    bias_all, xs, xr, os, orr, finals, wide_h, wide_l, qs, ks, vs, gates, chunk_bias,
    bias_send, bias_recv, x_send, x_recv, o_send, o_recv, final_send, final_recv,
):
    dap = lax.axis_index("dap")
    grp = lax.axis_index("grp")

    own = pl.ds(pl.multiple_of(dap * 16, 16), 16)
    pltpu.make_async_copy(bias_ref, bias_all.at[:, own, :], bias_recv.at[dap // 8]).start()

    def send_bias(k, carry):
        to = lax.rem(dap + k, 32)
        pltpu.make_async_remote_copy(
            src_ref=bias_ref, dst_ref=bias_all.at[:, own, :],
            send_sem=bias_send, recv_sem=bias_recv.at[dap // 8],
            device_id=(to, grp), device_id_type=MESH,
        ).start()
        return carry

    lax.fori_loop(1, 32, send_bias, 0)

    half = lax.rem(grp, 2)
    for s2 in range(2):
        a = x_ref[2 * s2, :, grp // 2]
        b = x_ref[2 * s2 + 1, :, grp // 2]
        first, second = merge_halves(a, b)
        xs[:, s2] = jnp.where(half == 0, first, second)
    pltpu.make_async_copy(xs.at[dap], xr.at[:, dap], x_recv).start()

    def send_x(k, carry):
        to = lax.rem(dap + k, 32)
        pltpu.make_async_remote_copy(
            src_ref=xs.at[to], dst_ref=xr.at[:, dap],
            send_sem=x_send, recv_sem=x_recv,
            device_id=(to, grp), device_id_type=MESH,
        ).start()
        return carry

    lax.fori_loop(1, 32, send_x, 0)

    final_to = finals.at[pl.ds(pl.multiple_of(grp * 64, 64), 64)]
    pltpu.make_async_copy(final_ref, final_to, final_recv).start()
    for k in range(1, 4):
        pltpu.make_async_remote_copy(
            src_ref=final_ref, dst_ref=final_to, send_sem=final_send, recv_sem=final_recv,
            device_id=(dap, lax.rem(grp + k, 4)), device_id_type=MESH,
        ).start()

    zero = jnp.zeros((256, 64), F32)
    q_w = weight_ref[0] * (LOG2E / math.sqrt(HEAD))
    k_w, v_w, g_w = weight_ref[1], weight_ref[2], weight_ref[3]
    wide = jnp.concatenate([q_w, q_w, q_w, zero, k_w, k_w, k_w, zero, v_w, v_w, g_w, g_w], axis=-1)
    high, low = split(wide)
    wide_h[...] = high
    wide_l[...] = low

    def project(s, carry):
        rows = split(normed(x_ref[s].reshape(512, 256)))
        out = dot3(rows, (wide_h[...], wide_l[...]))
        lane = lane_iota((512, 256))
        head = lax.rem(lane, 64) // HEAD
        q_hi, q_lo = split(out[:, 0:256])
        q = jnp.where((lane >= 64) & (lane < 128), q_lo.astype(F32), q_hi.astype(F32))
        k_hi, k_lo = split(out[:, 256:512])
        k = jnp.where((lane >= 128) & (lane < 192), k_lo.astype(F32), k_hi.astype(F32))
        ks[s] = k.astype(BF16)
        lane_v = lane_iota((512, 128))
        head_v = lax.rem(lane_v, 64) // HEAD
        v_hi, v_lo = split(out[:, 512:640])
        v = jnp.where(lane_v >= 64, v_lo.astype(F32), v_hi.astype(F32))
        for h in range(2):
            qs[s, h] = jnp.where(head == h, q, 0.0).astype(BF16)
            vs[s, pl.ds(512 * h, 512), 0:128] = jnp.where(head_v == h, v, 0.0).astype(BF16)
            vs[s, pl.ds(512 * h, 512), 128:256] = jnp.where(head_v == h, 1.0, 0.0).astype(BF16)
        gates[s] = jax.nn.sigmoid(out[:, 640:768])
        return carry

    lax.fori_loop(0, 4, project, 0)

    def attend(step, carry):
        chunk = lax.rem(step + dap // 8, 4)
        here = pl.ds(pl.multiple_of(chunk * 128, 128), 128)
        bias_here = bias_all.at[:, here, :]
        drain(bias_here, bias_recv.at[chunk])
        ids = ids_ref[...].astype(F32)
        own_ids = jnp.transpose(jnp.broadcast_to(ids_ref[:, here].astype(F32), (128, 128)))
        same = (jnp.concatenate([own_ids] * 4, axis=-1) == ids).astype(F32)
        for h in range(2):
            chunk_bias[h] = (bias_here[h] + offset_ref[h] * same) * LOG2E
        outs = []
        for s in range(4):
            highs, lows = [], []
            for h in range(2):
                logits = dot(qs[s, h, here, :], ks[s], NT) + chunk_bias[h]
                weights = jnp.exp2(logits - jnp.max(logits, axis=-1, keepdims=True))
                high, low = split(weights)
                highs.append(high)
                lows.append(low)
            v = vs[s]
            total = dot(jnp.concatenate(highs, axis=-1), v) + dot(jnp.concatenate(lows, axis=-1), v)
            top = total[:, 0:128]
            top = top + pltpu.roll(top, 64, axis=1)
            outs.append(top / total[:, 128:256] * gates[s, here, :])
        left_lanes = lane_iota((128, 128)) < 64
        pair = [jnp.where(left_lanes, outs[s1], outs[2 + s1]).reshape(16, 8, 128) for s1 in range(2)]
        first, second = merge_halves(*pair)
        tiles = pl.ds(chunk * 16, 16)
        os[tiles, 0] = first
        os[tiles, 1] = second

        def send_o(k, carry):
            block = lax.rem(k + dap * 4 + grp, 32) + chunk * 32
            to_dap, to_grp = block // 4, lax.rem(block, 4)
            mine = (to_dap == dap) & (to_grp == grp)
            src = os.at[block // 2, lax.rem(block, 2)]
            dst = orr.at[grp * 32 + dap]

            @pl.when(mine)
            def _():
                pltpu.make_async_copy(src, dst, o_recv).start()

            @pl.when(jnp.logical_not(mine))
            def _():
                pltpu.make_async_remote_copy(
                    src_ref=src, dst_ref=dst, send_sem=o_send, recv_sem=o_recv,
                    device_id=(to_dap, to_grp), device_id_type=MESH,
                ).start()

            return carry

        lax.fori_loop(0, 32, send_o, 0)
        return carry

    lax.fori_loop(0, 4, attend, 0)

    drain(bias_all.at[:, 0:496, :], bias_send)
    drain(xs.at[0:31], x_send)
    drain(orr.at[0:127], o_send)
    drain(xr, x_recv)
    drain(orr, o_recv)
    drain(finals.at[0:192], final_send)
    drain(finals, final_recv)
    xr_ref[...] = xr[...]
    or_ref[...] = orr[...]
    finals_ref[...] = finals[...]


def column_kernel(
    xr_ref, or_ref, row_final_ref, live_ref, vertical_ref, final_ref, expand_ref, shrink_ref, tensor_ref,
    revised_ref, left_ref, right_ref,
    msa, proj, attended, units,
):
    zero = jnp.zeros((64, 256), F32)
    parts = split(jnp.concatenate([or_ref[pl.ds(32 * g, 32)].reshape(256, 128) for g in range(4)], axis=-1))
    for s2 in range(2):
        pieces = []
        for g in range(4):
            own = row_final_ref[64 * g:64 * g + 64, :]
            pieces += [own, zero] if s2 == 0 else [zero, own]
        out = dot3(parts, split(jnp.concatenate(pieces, axis=0)))
        msa[pl.ds(256 * s2, 256), :] = xr_ref[s2].reshape(256, 256) + out

    rows = split(normed(msa[...]))
    for m in range(4):
        w = vertical_ref[m]
        if m == 0:
            w = w * (LOG2E / math.sqrt(HEAD))
        out = dot3(rows, split(w))
        for part in range(2):
            proj[2 * m + part] = out[:, 128 * part:128 * part + 128]

    at = lax.broadcasted_iota(jnp.int32, (128, 128), 0)
    to = lax.broadcasted_iota(jnp.int32, (128, 128), 1)
    order = (at == 4 * lax.rem(to // 2, 32) + 2 * (to // 64) + lax.rem(to, 2)).astype(BF16)
    live = dot(live_ref[...].astype(F32).astype(BF16), order)
    live_total = jnp.sum(live)
    mask = (live - 1.0) * (1e9 * LOG2E)

    lane = lane_iota((128, 128))
    for r in range(4):
        for part in range(2):
            q, k, v, g = (proj[2 * m + part, pl.ds(r, 128, stride=4), :] for m in range(4))
            q_h, q_l = split(q)
            k_h, k_l = split(k)
            v_h, v_l = split(v)
            keys = jnp.concatenate([k_h, k_h, k_l], axis=-1)
            wide_q, wide_v = [], []
            for h in range(4):
                mine = lane // HEAD == h
                none = jnp.zeros((128, 128), BF16)
                qm_h, qm_l = jnp.where(mine, q_h, none), jnp.where(mine, q_l, none)
                wide_q.append(jnp.concatenate([qm_h, qm_l, qm_h], axis=-1))
                wide_v.append(jnp.concatenate(
                    [jnp.where(mine, v_h, none), jnp.where(mine, v_l, none), mine.astype(BF16)], axis=-1))
            logits = dot(jnp.concatenate(wide_q, axis=0), keys, NT) + mask
            weights = jnp.exp2(logits - jnp.max(logits, axis=-1, keepdims=True))
            high, low = split(weights)
            values = jnp.concatenate(wide_v, axis=0)

            def heads_in_lanes(a):
                return jnp.concatenate([a[128 * h:128 * h + 128] for h in range(4)], axis=-1)

            total = dot(heads_in_lanes(high), values) + dot(heads_in_lanes(low), values)
            out = (total[:, 0:128] + total[:, 128:256]) / total[:, 256:384]
            attended[part, pl.ds(r, 128, stride=4), :] = out * jax.nn.sigmoid(g)

    current = msa[...] + dot3(split(jnp.concatenate([attended[0], attended[1]], axis=-1)), split(final_ref[...]))
    hidden = jnp.maximum(dot3(split(normed(current)), split(expand_ref[...])), 0.0)
    revised = current + dot3(split(hidden), split(shrink_ref[...]))
    for s2 in range(2):
        revised_ref[:, s2] = revised[256 * s2:256 * s2 + 256].reshape(32, 8, 256)

    unit = normed(revised)
    for part in range(2):
        units[part] = unit[:, 128 * part:128 * part + 128]
    narrow = jnp.concatenate([tensor_ref[0], tensor_ref[1], jnp.zeros((256, 64), F32)], axis=-1)
    narrow = split(jnp.transpose(narrow)[0:64])
    for r in range(4):
        both = dot3(narrow, split(jnp.concatenate([units[part, pl.ds(r, 128, stride=4), :] for part in range(2)], axis=-1)), NT)
        left_ref[pl.ds(32 * r, 32), :] = both[0:32] * (live / live_total)
        right_ref[pl.ds(r, 32, stride=4), :] = both[32:64] * live


def pair_kernel(
    left_ref, right_ref, couple_ref, out_ref,
    left_all, right_all, right_sorted, outer_h, outer_l, couple_h, couple_l,
    left_send, left_recv, right_send, right_recv,
):
    dap = lax.axis_index("dap")
    grp = lax.axis_index("grp")

    left_to = left_all.at[pl.ds(pl.multiple_of(grp * 128, 128), 128)]
    pltpu.make_async_copy(left_ref, left_to, left_recv).start()
    for k in range(1, 4):
        pltpu.make_async_remote_copy(
            src_ref=left_ref, dst_ref=left_to, send_sem=left_send, recv_sem=left_recv,
            device_id=(dap, lax.rem(grp + k, 4)), device_id_type=MESH,
        ).start()

    to_grp = dap // 8
    slot = lax.rem(dap, 8) * 4 + grp
    right_to = right_all.at[slot]

    def send_right(k, carry):
        to = lax.rem(dap + k, 32)
        mine = (to == dap) & (to_grp == grp)

        @pl.when(mine)
        def _():
            pltpu.make_async_copy(right_ref, right_to, right_recv).start()

        @pl.when(jnp.logical_not(mine))
        def _():
            pltpu.make_async_remote_copy(
                src_ref=right_ref, dst_ref=right_to, send_sem=right_send, recv_sem=right_recv,
                device_id=(to, to_grp), device_id_type=MESH,
            ).start()

        return carry

    lax.fori_loop(0, 32, send_right, 0)

    for e in range(8):
        rows = jnp.concatenate([couple_ref[pl.ds(4 * e + i, 32, stride=32), :] for i in range(4)], axis=0)
        high, low = split(jnp.transpose(rows))
        couple_h[:, 128 * e:128 * e + 128] = high
        couple_l[:, 128 * e:128 * e + 128] = low

    drain(left_all, left_recv)
    drain(right_all, right_recv)
    left_h, left_l = split(left_all[...])
    left_wide = jnp.concatenate([left_h, left_l, left_h], axis=-1)

    def sort(e2, carry):
        for t in range(16):
            first, second = merge_halves(
                right_all[2 * t, pl.ds(e2 * 8, 8), :], right_all[2 * t + 1, pl.ds(e2 * 8, 8), :])
            right_sorted[2 * e2, pl.ds(8 * t, 8), :] = first
            right_sorted[2 * e2 + 1, pl.ds(8 * t, 8), :] = second
        return carry

    lax.fori_loop(0, 16, sort, 0)

    def outer(e2, carry):
        high, low = split(right_sorted[pl.ds(2 * e2, 2)].reshape(256, 128))
        right_wide = jnp.concatenate([high, high, low], axis=-1)
        product = dot(left_wide, right_wide, NT)
        high, low = split(product)
        for i in range(16):
            for e1 in range(2):
                at = pl.ds(pl.multiple_of(64 * e2 + 32 * e1, 32), 32)
                lanes = slice(128 * (i % 2), 128 * (i % 2) + 128)
                rows, cols = slice(32 * i, 32 * i + 32), slice(128 * e1, 128 * e1 + 128)
                outer_h[i // 2, at, lanes] = high[rows, cols]
                outer_l[i // 2, at, lanes] = low[rows, cols]
        return carry

    lax.fori_loop(0, 16, outer, 0)

    def finish(i2, carry):
        out = dot3((couple_h[...], couple_l[...]), (outer_h[i2], outer_l[i2]))
        for i1 in range(2):
            out_ref[2 * i2 + i1] = jnp.transpose(out[:, 128 * i1:128 * i1 + 128])
        return carry

    lax.fori_loop(0, 8, finish, 0)
    drain(left_all.at[0:384], left_send)
    own = to_grp == grp

    @pl.when(own)
    def _():
        drain(right_all.at[0:31], right_send)

    @pl.when(jnp.logical_not(own))
    def _():
        drain(right_all, right_send)


VM = pl.BlockSpec(memory_space=pltpu.VMEM)
SM = pl.BlockSpec(memory_space=pltpu.SMEM)
LIMIT = 56 * 1024 * 1024


def body(
    homolog_stack,
    couple_score_offset,
    strand_identity,
    strand_score_offset,
    homolog_presence,
    horizontal_matrix,
    horizontal_final_matrix,
    vertical_matrix,
    vertical_final_matrix,
    expand_matrix,
    shrink_matrix,
    tensor_matrix,
    couple_matrix,
):
    shape = jax.ShapeDtypeStruct
    dma = pltpu.SemaphoreType.DMA
    moved_x, moved_o, finals = pl.pallas_call(
        row_kernel,
        out_shape=[shape((2, 32, 8, 256), F32), shape((128, 8, 128), F32), shape((256, 256), F32)],
        in_specs=[VM, VM, VM, SM, VM, VM],
        out_specs=[VM] * 3,
        scratch_shapes=[
            pltpu.VMEM((2, 512, 512), F32),
            pltpu.VMEM((32, 2, 8, 256), F32),
            pltpu.VMEM((2, 32, 8, 256), F32),
            pltpu.VMEM((64, 2, 8, 128), F32),
            pltpu.VMEM((128, 8, 128), F32),
            pltpu.VMEM((256, 256), F32),
            pltpu.VMEM((256, 768), BF16),
            pltpu.VMEM((256, 768), BF16),
            pltpu.VMEM((4, 2, 512, 256), BF16),
            pltpu.VMEM((4, 512, 256), BF16),
            pltpu.VMEM((4, 1024, 256), BF16),
            pltpu.VMEM((4, 512, 128), F32),
            pltpu.VMEM((2, 128, 512), F32),
            dma, dma((4,)), dma, dma, dma, dma, dma, dma,
        ],
        compiler_params=pltpu.CompilerParams(has_side_effects=True, vmem_limit_bytes=LIMIT),
        name="row_attention",
    )(
        homolog_stack.reshape(4, 32, 2, 8, 256),
        couple_score_offset,
        strand_identity.reshape(1, 512),
        strand_score_offset,
        horizontal_matrix,
        horizontal_final_matrix,
    )
    revised, left, right = pl.pallas_call(
        column_kernel,
        out_shape=[shape((32, 2, 8, 256), F32), shape((128, 128), F32), shape((128, 128), F32)],
        in_specs=[VM] * 9,
        out_specs=[VM] * 3,
        scratch_shapes=[
            pltpu.VMEM((512, 256), F32),
            pltpu.VMEM((8, 512, 128), F32),
            pltpu.VMEM((2, 512, 128), F32),
            pltpu.VMEM((2, 512, 128), F32),
        ],
        compiler_params=pltpu.CompilerParams(vmem_limit_bytes=LIMIT),
        name="column_section",
    )(
        moved_x, moved_o, finals, homolog_presence.reshape(1, 128), vertical_matrix, vertical_final_matrix,
        expand_matrix, shrink_matrix, tensor_matrix,
    )
    pair = pl.pallas_call(
        pair_kernel,
        out_shape=shape((16, 128, 128), F32),
        in_specs=[VM] * 3,
        out_specs=VM,
        scratch_shapes=[
            pltpu.VMEM((512, 128), F32),
            pltpu.VMEM((32, 128, 128), F32),
            pltpu.VMEM((32, 128, 128), F32),
            pltpu.VMEM((8, 1024, 256), BF16),
            pltpu.VMEM((8, 1024, 256), BF16),
            pltpu.VMEM((128, 1024), BF16),
            pltpu.VMEM((128, 1024), BF16),
            dma, dma, dma, dma,
        ],
        compiler_params=pltpu.CompilerParams(has_side_effects=True, vmem_limit_bytes=LIMIT),
        name="pair_update",
    )(left, right, couple_matrix)
    return revised.reshape(128, 4, 256), pair


def solution(mesh):
    return jax.shard_map(
        body,
        mesh=mesh,
        in_specs=(
            P("dap", None, None),
            P("grp", "dap", None),
            P(),
            P("grp"),
            P(),
            P(None, None, "grp"),
            P("grp", None),
            P(),
            P(),
            P(),
            P(),
            P(),
            P(),
        ),
        out_specs=(P(None, ("dap", "grp"), None), P("dap", "grp", None)),
        check_vma=False,
    )
```

time: 611 us -> 160 us (0.26)
  waiting for transfers between devices: 408 us -> 0 us
  Pallas kernels: 0 us -> 149 us
  matrix products: 68.1 us -> 0 us
  local copies, waits for them, and re-layouts: 46 us -> 7.91 us
  starting transfers between devices: 30.3 us -> 0 us
  other arithmetic: 25.9 us -> 0 us
  between operations: 14.5 us -> 0.65 us
  blocking collectives: 9.9 us -> 0 us
    all_gather x2 -> x0, waiting for transfers between devices: 276 us -> none  [the longest x1 147 us: body(): right_wide = lax.all_gather(right_rows, 'dap', axis=1, tiled=True)]
    pallas_call x0 -> x3, Pallas kernels: none -> 149 us  [the longest x1 72.7 us: body(): pl.pallas_call(row_kernel, out_shape=[shape((2, 32, 8, 256), F32), shape(...]
    psum x1 -> x0, waiting for transfers between devices: 80.1 us -> none  [body(): accumulated_tensor = lax.psum(partial_rows, 'grp')]
    dot_general x22 -> x0, matrix products: 68.1 us -> none  [the longest x1 15.7 us: outer_project(): jnp.dot(flat, couple_matrix, precision=HIGH_PRECISION)]
    all_to_all x2 -> x0, waiting for transfers between devices: 52.1 us -> none  [the longest x1 26.9 us: body(): lax.all_to_all(revised_tensor, 'dap', split_axis=1, concat_axis=0, tiled=...]
    all_to_all x2 -> x0, starting transfers between devices: 29.9 us -> none  [the longest x1 22.8 us: body(): lax.all_to_all(right_wide, 'grp', split_axis=1, concat_axis=0, tiled=True)]
    unnamed x45 -> x3, local copies, waits for them, and re-layouts: 19.3 us -> 5.93 us
    all_gather x1 -> x0, blocking collectives: 9.9 us -> none  [body(): gathered = lax.all_gather(joined_parts, 'grp', axis=1, tiled=True)]
  transfers between devices with their start and end apart: 5 -> 0, of which waited for: 5 -> 0; matrix products, arithmetic and copies ran while one was open for 2% -> 0% of each run, Pallas kernels for 0% -> 0%
where the time goes in v1:
time: 160 us; the launch traced here: 158 us
  Pallas kernels  149 us (93%)
  local copies, waits for them, and re-layouts  7.91 us (5%)
    pallas_call x1, Pallas kernels, body(): pl.pallas_call(row_kernel, out_shape=[shape((2, 32, 8, 256), F32), shape(...  72.7 us
    pallas_call x1, Pallas kernels, body(): pl.pallas_call(pair_kernel, out_shape=shape((16, 128, 128), F32), in_spec...  63.8 us
    pallas_call x1, Pallas kernels, body(): pl.pallas_call(column_kernel, out_shape=[shape((32, 2, 8, 256), F32), sha...  12.5 us
    unnamed x3, local copies, waits for them, and re-layouts  5.93 us

profile of v1, /device:TPU:1, one launch (start us, length us, event | category | flops | bytes accessed | tf_op | source)
XLA Modules:
  0.0 157.6 jit_solution(7972993627197059860)
XLA Ops:
  0.6 1.7 %copy.16.tensor_ref = f32[2,256,32]{2,1,0:T(8,128)} copy(f32[2,256,32]{1,2,0:T(8,128)} %param.24) | data formatting | bytes 131072 | tf_op args[11]
  2.3 1.9 %copy.15.weight_ref = f32[4,256,64]{2,1,0:T(8,128)} copy(f32[4,256,64]{1,2,0:T(8,128)} %param.18) | data formatting | bytes 524288 | tf_op args[5]
  4.3 72.7 %row_attention.1 = (f32[2,32,8,256]{3,2,1,0:T(8,128)}, f32[128,8,128]{2,1,0:T(8,128)}, f32[256,256]{1,0:T(8,128)}) custom-call(f32[4,32,2,8,256]{4,3,2,1,0:T(8,128)} %bitcast.5, f32[2,16,512]{2,1,0:T(8,128)} %bias_ref.1, s32[1,512]{1,0:T(1,128)} %bitcast.6, f32[2]{0:T(128)} %offset_ref.1, f32[4,256,64]{2,1,0:T(8,128)} %copy.15.weight_ref, f32[64,256]{1,0:T(8,128)} %final_ref.2), custom_call_target="tpu_custom_call" | custom-call | tf_op jit(solution)/shard_map/row_attention/pallas_call | solution.py:396
  77.0 12.5 %column_section.1 = (f32[32,2,8,256]{3,2,1,0:T(8,128)}, f32[128,128]{1,0:T(8,128)}, f32[128,128]{1,0:T(8,128)}) custom-call(f32[2,32,8,256]{3,2,1,0:T(8,128)} %get-tuple-element.8.xr_ref, f32[128,8,128]{2,1,0:T(8,128)} %get-tuple-element.9.or_ref, f32[256,256]{1,0:T(8,128)} %get-tuple-element.10.row_final_ref, s32[1,128]{1,0:T(1,128)} %bitcast.7, ...), custom_call_target="tpu_custom_call" | custom-call | tf_op jit(solution)/shard_map/column_section/pallas_call | solution.py:427
  89.5 2.0 %reshape.19 = f32[128,4,256]{2,1,0:T(4,128)} reshape(f32[32,2,8,256]{3,2,1,0:T(8,128)} %get-tuple-element.11) | data formatting | bytes 1048576 | tf_op jit(solution)/shard_map/reshape | solution.py:462
  91.4 63.8 %pair_update.1 = f32[16,128,128]{2,1,0:T(8,128)} custom-call(f32[128,128]{1,0:T(8,128)} %get-tuple-element.12.left_ref, f32[128,128]{1,0:T(8,128)} %get-tuple-element.13.right_ref, f32[1024,128]{1,0:T(8,128)} %couple_ref.1), custom_call_target="tpu_custom_call" | custom-call | tf_op jit(solution)/shard_map/pair_update/pallas_call | solution.py:444
  155.3 2.3 %copy.18 = f32[16,128,128]{2,1,0:T(8,128)} copy(f32[16,128,128]{2,1,0:T(8,128)} %pair_update.1) | data formatting | bytes 2097152

commit v2 on v1

v2 whole, which is shorter than its diff:
```python
import functools
import math

import jax
import jax.numpy as jnp
from jax import lax
from jax.experimental import pallas as pl
from jax.experimental.pallas import tpu as pltpu
from jax.sharding import PartitionSpec as P

F32 = jnp.float32
BF16 = jnp.bfloat16
MESH = pl.DeviceIdType.MESH
HEAD = 32
LOG2E = math.log2(math.e)
NN = (((1,), (0,)), ((), ()))
NT = (((1,), (1,)), ((), ()))


def split(a):
    high = a.astype(BF16)
    return high, (a - high.astype(F32)).astype(BF16)


def dot(a, b, dims=NN):
    return lax.dot_general(a, b, dims, preferred_element_type=F32)


def dot3(a, b, dims=NN):
    return dot(a[0], b[0], dims) + (dot(a[0], b[1], dims) + dot(a[1], b[0], dims))


def normed(rows):
    center = rows - jnp.mean(rows, axis=-1, keepdims=True)
    spread = jnp.mean(center * center, axis=-1, keepdims=True)
    return center * lax.rsqrt(spread + 1e-05)


def merge_halves(a, b):
    upper = lax.broadcasted_iota(jnp.int32, a.shape, a.ndim - 2) < 4
    first = jnp.where(upper, a, pltpu.roll(b, 4, axis=b.ndim - 2))
    second = jnp.where(upper, pltpu.roll(a, 4, axis=a.ndim - 2), b)
    return first, second


def lane_iota(shape):
    return lax.broadcasted_iota(jnp.int32, shape, len(shape) - 1)


def drain(ref, sem):
    pltpu.make_async_copy(ref, ref, sem).wait()


def signal(sem, device):
    pl.semaphore_signal(sem, inc=1, device_id=device, device_id_type=MESH)


def send(src, dst, send_sem, recv_sem, device):
    pltpu.make_async_remote_copy(
        src_ref=src, dst_ref=dst, send_sem=send_sem, recv_sem=recv_sem,
        device_id=device, device_id_type=MESH,
    ).start()


def kernel(
    x_ref, bias_ref, ids_ref, offset_ref, weight_ref, final_in_ref, live_ref, vertical_ref, final_ref,
    expand_ref, shrink_ref, tensor_ref, couple_ref,
    revised_ref, out_ref,
    bias_all, xs, xr, os, orr, finals, wide_h, wide_l, qs, ks, vs, gates, ids_col, chunk_bias,
    msa, proj, attended, units,
    left_own, right_own, left_all, right_all, right_sorted, outer_h, outer_l, couple_h, couple_l,
    bias_send, bias_recv, x_send, x_recv, o_send, o_recv, final_send, final_recv,
    left_send, left_recv, right_send, right_recv, near_z, near_x, near_y,
):
    dap = lax.axis_index("dap")
    grp = lax.axis_index("grp")
    y, x, z = dap // 16, lax.rem(dap // 4, 4), lax.rem(dap, 4)
    x_at = [lax.rem(x + i, 4) for i in range(4)]
    z_at = [lax.rem(z + i, 4) for i in range(4)]

    def along_x(i):
        return y * 16 + x_at[i % 4] * 4 + z, grp

    def along_z(i):
        return y * 16 + x * 4 + z_at[i % 4], grp

    across_y = ((1 - y) * 16 + x * 4 + z, grp)

    barrier = pltpu.get_barrier_semaphore()
    for i in range(1, 4):
        signal(barrier, along_x(i))
        signal(barrier, along_z(i))
        signal(barrier, (dap, lax.rem(grp + i, 4)))
    signal(barrier, across_y)

    zero = jnp.zeros((64, 256), F32)
    q_w = weight_ref[0] * (LOG2E / math.sqrt(HEAD))
    k_w, v_w, g_w = weight_ref[1], weight_ref[2], weight_ref[3]
    for at, parts in ((0, (q_w, q_w, q_w, zero)), (256, (k_w, k_w, k_w, zero)), (512, (v_w, v_w, g_w, g_w))):
        high, low = split(jnp.transpose(jnp.concatenate(parts, axis=0)))
        wide_h[:, at:at + 256] = high
        wide_l[:, at:at + 256] = low
    pl.semaphore_wait(barrier, 10)

    def unit(p, i, j, h=None):
        a, b = (x_at[j % 4], z_at[i % 4]) if p == 0 else (x_at[i % 4], z_at[j % 4])
        return bias_all.at[p, a, b] if h is None else bias_all.at[p, a, b, h]

    def line(p, j, h):
        return bias_all.at[0, x_at[j % 4], :, h] if p == 0 else bias_all.at[1, :, z_at[j % 4], h]

    def first_axis(p, i):
        return along_z(i) if p == 0 else along_x(i)

    def second_axis(p, i):
        return along_x(i) if p == 0 else along_z(i)

    steps = ((0, 1), (1, -1))
    own = bias_all.at[y, x, z]
    send(bias_ref, own, bias_send, bias_recv.at[0], across_y)
    pltpu.make_async_copy(bias_ref, own, bias_recv.at[21]).start()
    for i in range(1, 4):
        signal(near_z, along_z(i))
    drain(bias_ref, bias_recv.at[21])

    def spread(p):
        for k, sign in steps:
            send(unit(p, 0, 0), unit(p, 0, 0), bias_send, bias_recv.at[1 + 10 * p + k], first_axis(p, sign))

    for p in range(2):
        @pl.when(y == p)
        def _():
            spread(p)

    def project(s):
        rows = split(normed(x_ref[s].reshape(512, 256)))
        out = dot3(rows, (wide_h[...], wide_l[...]))
        lane = lane_iota((512, 256))
        head = lax.rem(lane, 64) // HEAD
        q_hi, q_lo = split(out[:, 0:256])
        q = jnp.where((lane >= 64) & (lane < 128), q_lo.astype(F32), q_hi.astype(F32))
        k_hi, k_lo = split(out[:, 256:512])
        k = jnp.where((lane >= 128) & (lane < 192), k_lo.astype(F32), k_hi.astype(F32))
        ks[s] = k.astype(BF16)
        lane_v = lane_iota((512, 128))
        head_v = lax.rem(lane_v, 64) // HEAD
        v_hi, v_lo = split(out[:, 512:640])
        v = jnp.where(lane_v >= 64, v_lo.astype(F32), v_hi.astype(F32))
        for h in range(2):
            qs[s, h] = jnp.where(head == h, q, 0.0).astype(BF16).reshape(32, 16, 256)
            vs[s, pl.ds(512 * h, 512), 0:128] = jnp.where(head_v == h, v, 0.0).astype(BF16)
            vs[s, pl.ds(512 * h, 512), 128:256] = jnp.where(head_v == h, 1.0, 0.0).astype(BF16)
        gates[s] = jax.nn.sigmoid(out[:, 640:768]).reshape(32, 16, 128)

    def project_and(s, carry):
        project(s)

        @pl.when(s == 0)
        def _():
            pl.semaphore_wait(near_z, 3)
            for i in range(1, 4):
                signal(near_x, along_x(i))
            drain(bias_ref, bias_recv.at[0])
            for p in range(2):
                @pl.when(y == 1 - p)
                def _():
                    spread(p)

        @pl.when(s == 1)
        def _():
            for p in range(2):
                for k, sign in steps:
                    drain(bias_ref, bias_recv.at[1 + 10 * p + k])
                    send(unit(p, -sign, 0, k), unit(p, -sign, 0, k), bias_send,
                         bias_recv.at[3 + 10 * p + k], first_axis(p, sign))
            pl.semaphore_wait(near_x, 3)
            signal(near_y, across_y)

        @pl.when(s == 2)
        def _():
            for p in range(2):
                for k in range(2):
                    drain(bias_ref.at[0], bias_recv.at[3 + 10 * p + k])
                for k, sign in steps:
                    send(line(p, 0, k), line(p, 0, k), bias_send, bias_recv.at[5 + 10 * p + k], second_axis(p, sign))
                for k, sign in steps:
                    send(line(p, 0, 1 - k), line(p, 0, 1 - k), bias_send,
                         bias_recv.at[7 + 10 * p + k], second_axis(p, sign))

        return carry

    lax.fori_loop(0, 4, project_and, 0)

    half = lax.rem(grp, 2)
    for s2 in range(2):
        first, second = merge_halves(x_ref[2 * s2, :, grp // 2], x_ref[2 * s2 + 1, :, grp // 2])
        xs[:, s2] = jnp.where(half == 0, first, second)
    for i in range(4):
        block = jnp.broadcast_to(ids_ref[:, 128 * i:128 * i + 128].astype(F32), (128, 128))
        ids_col[8 * i:8 * i + 8] = jnp.transpose(block).reshape(8, 16, 128)
    pl.semaphore_wait(near_y, 1)

    def attend(step, carry):
        turn = step + step // 2 - 2 * (step // 3)
        x_now, z_now = lax.rem(x + turn, 4), lax.rem(z + turn, 4)

        @pl.when(step == 1)
        def _():
            for p in range(2):
                for k, sign in steps:
                    drain(line(0, 0, 0), bias_recv.at[5 + 10 * p + k])
                    send(line(p, -sign, k), line(p, -sign, k), bias_send,
                         bias_recv.at[9 + 10 * p + k], second_axis(p, sign))
            pltpu.make_async_copy(xs.at[dap], xr.at[:, dap], x_recv).start()

            def send_x(k, carry):
                to = lax.rem(dap + k, 32)
                send(xs.at[to], xr.at[:, dap], x_send, x_recv, (to, grp))
                return carry

            lax.fori_loop(1, 32, send_x, 0)
            final_to = finals.at[pl.ds(pl.multiple_of(grp * 64, 64), 64)]
            pltpu.make_async_copy(final_in_ref, final_to, final_recv).start()
            for k in range(1, 4):
                send(final_in_ref, final_to, final_send, final_recv, (dap, lax.rem(grp + k, 4)))
            for p in range(2):
                drain(line(0, 0, 0), bias_recv.at[7 + 10 * p + 1])

        @pl.when(step == 2)
        def _():
            for p in range(2):
                drain(line(0, 0, 0), bias_recv.at[7 + 10 * p])

        @pl.when(step == 3)
        def _():
            for p in range(2):
                for k in range(2):
                    drain(line(0, 0, 0), bias_recv.at[9 + 10 * p + k])

        def rows_of(ref, *lead):
            shape = ref.shape[-2:]
            upper = ref[(*lead, pl.ds(4 * x_now, 4))].reshape(64, shape[-1])
            return jnp.concatenate([upper] + [ref[(*lead, 16 + 4 * i + z_now)] for i in range(4)], axis=0)

        own_ids = rows_of(ids_col)
        same = (jnp.concatenate([own_ids] * 4, axis=-1) == ids_ref[...].astype(F32)).astype(F32)
        for h in range(2):
            here = jnp.concatenate(
                [bias_all[0, x_now, :, h].reshape(64, 512), bias_all[1, :, z_now, h].reshape(64, 512)], axis=0)
            chunk_bias[h] = (here + offset_ref[h] * same) * LOG2E
        outs = []
        for s in range(4):
            highs, lows = [], []
            for h in range(2):
                logits = dot(rows_of(qs, s, h), ks[s], NT) + chunk_bias[h]
                weights = jnp.exp2(logits - jnp.max(logits, axis=-1, keepdims=True))
                high, low = split(weights)
                highs.append(high)
                lows.append(low)
            v = vs[s]
            total = dot(jnp.concatenate(highs, axis=-1), v) + dot(jnp.concatenate(lows, axis=-1), v)
            top = total[:, 0:128]
            top = top + pltpu.roll(top, 64, axis=1)
            outs.append(top / total[:, 128:256] * rows_of(gates, s))
        left_lanes = lane_iota((128, 128)) < 64
        pair = [jnp.where(left_lanes, outs[s1], outs[2 + s1]).reshape(16, 8, 128) for s1 in range(2)]
        for side, tiles in enumerate(merge_halves(*pair)):
            os[pl.ds(8 * x_now, 8), side] = tiles[0:8]
            for i in range(4):
                os[pl.ds(32 + 8 * i + 2 * z_now, 2), side] = tiles[8 + 2 * i:10 + 2 * i]

        def send_o(k, carry):
            turned = lax.rem(k + 4 * (x + z) + grp, 32)
            low_half = 1 - turned // 16
            place = lax.rem(turned // 4, 4)
            to_grp = lax.rem(turned, 4)
            to_dap = low_half * (4 * x_now + place) + (1 - low_half) * (16 + 4 * place + z_now)
            mine = (to_dap == dap) & (to_grp == grp)
            src = os.at[2 * to_dap + to_grp // 2, lax.rem(to_grp, 2)]
            dst = orr.at[grp * 32 + dap]

            @pl.when(mine)
            def _():
                pltpu.make_async_copy(src, dst, o_recv).start()

            @pl.when(jnp.logical_not(mine))
            def _():
                send(src, dst, o_send, o_recv, (to_dap, to_grp))

            return carry

        lax.fori_loop(0, 32, send_o, 0)
        return carry

    lax.fori_loop(0, 4, attend, 0)

    for e in range(8):
        rows = jnp.concatenate([couple_ref[pl.ds(4 * e + i, 32, stride=32), :] for i in range(4)], axis=0)
        high, low = split(jnp.transpose(rows))
        couple_h[:, 128 * e:128 * e + 128] = high
        couple_l[:, 128 * e:128 * e + 128] = low

    drain(xr, x_recv)
    drain(finals, final_recv)
    drain(orr, o_recv)

    zero = jnp.zeros((64, 256), F32)
    parts = split(jnp.concatenate([orr[pl.ds(32 * g, 32)].reshape(256, 128) for g in range(4)], axis=-1))
    for s2 in range(2):
        pieces = []
        for g in range(4):
            own = finals[64 * g:64 * g + 64, :]
            pieces += [own, zero] if s2 == 0 else [zero, own]
        out = dot3(parts, split(jnp.concatenate(pieces, axis=0)))
        msa[pl.ds(256 * s2, 256), :] = xr[s2].reshape(256, 256) + out

    rows = split(normed(msa[...]))
    for m in range(4):
        w = vertical_ref[m]
        if m == 0:
            w = w * (LOG2E / math.sqrt(HEAD))
        out = dot3(rows, split(w))
        for part in range(2):
            proj[2 * m + part] = out[:, 128 * part:128 * part + 128]

    at = lax.broadcasted_iota(jnp.int32, (128, 128), 0)
    to = lax.broadcasted_iota(jnp.int32, (128, 128), 1)
    order = (at == 4 * lax.rem(to // 2, 32) + 2 * (to // 64) + lax.rem(to, 2)).astype(BF16)
    live = dot(live_ref[...].astype(F32).astype(BF16), order)
    live_total = jnp.sum(live)
    mask = (live - 1.0) * (1e9 * LOG2E)

    lane = lane_iota((128, 128))
    for r in range(4):
        for part in range(2):
            q, k, v, g = (proj[2 * m + part, pl.ds(r, 128, stride=4), :] for m in range(4))
            q_h, q_l = split(q)
            k_h, k_l = split(k)
            v_h, v_l = split(v)
            keys = jnp.concatenate([k_h, k_h, k_l], axis=-1)
            wide_q, wide_v = [], []
            for h in range(4):
                mine = lane // HEAD == h
                none = jnp.zeros((128, 128), BF16)
                qm_h, qm_l = jnp.where(mine, q_h, none), jnp.where(mine, q_l, none)
                wide_q.append(jnp.concatenate([qm_h, qm_l, qm_h], axis=-1))
                wide_v.append(jnp.concatenate(
                    [jnp.where(mine, v_h, none), jnp.where(mine, v_l, none), mine.astype(BF16)], axis=-1))
            logits = dot(jnp.concatenate(wide_q, axis=0), keys, NT) + mask
            weights = jnp.exp2(logits - jnp.max(logits, axis=-1, keepdims=True))
            high, low = split(weights)
            values = jnp.concatenate(wide_v, axis=0)

            def heads_in_lanes(a):
                return jnp.concatenate([a[128 * h:128 * h + 128] for h in range(4)], axis=-1)

            total = dot(heads_in_lanes(high), values) + dot(heads_in_lanes(low), values)
            out = (total[:, 0:128] + total[:, 128:256]) / total[:, 256:384]
            attended[part, pl.ds(r, 128, stride=4), :] = out * jax.nn.sigmoid(g)

    current = msa[...] + dot3(split(jnp.concatenate([attended[0], attended[1]], axis=-1)), split(final_ref[...]))
    hidden = jnp.maximum(dot3(split(normed(current)), split(expand_ref[...])), 0.0)
    revised = current + dot3(split(hidden), split(shrink_ref[...]))
    for s2 in range(2):
        revised_ref[:, s2] = revised[256 * s2:256 * s2 + 256].reshape(32, 8, 256)

    unit = normed(revised)
    for part in range(2):
        units[part] = unit[:, 128 * part:128 * part + 128]
    narrow = split(tensor_ref[...].reshape(64, 256))
    for r in range(4):
        both = dot3(narrow, split(jnp.concatenate([units[part, pl.ds(r, 128, stride=4), :] for part in range(2)], axis=-1)), NT)
        left_own[pl.ds(32 * r, 32), :] = both[0:32] * (live / live_total)
        right_own[pl.ds(r, 32, stride=4), :] = both[32:64] * live

    left_to = left_all.at[pl.ds(pl.multiple_of(grp * 128, 128), 128)]
    pltpu.make_async_copy(left_own, left_to, left_recv).start()
    for k in range(1, 4):
        send(left_own, left_to, left_send, left_recv, (dap, lax.rem(grp + k, 4)))

    pass_grp = 2 * y + x // 2
    near = lax.rem(x, 2)
    slot = right_all.at[near, z, grp]
    for y_to in range(2):
        mine = (y == y_to) & (grp == pass_grp)

        @pl.when(mine)
        def _():
            pltpu.make_async_copy(right_own, slot, right_recv.at[0]).start()

        @pl.when(jnp.logical_not(mine))
        def _():
            send(right_own, slot, right_send, right_recv.at[0], (y_to * 16 + x * 4 + z, pass_grp))

    passing = lax.rem(grp, 2) == x // 2
    to_same = (y * 16 + lax.rem(x + 1 + 2 * near, 4) * 4 + z, grp)
    to_other = (y * 16 + lax.rem(x + 3 + 2 * near, 4) * 4 + z, grp)
    first_rows, last_rows = pl.ds(0, 64), pl.ds(64, 64)

    def by_x(p, row, part=None):
        rows = first_rows if p == 0 else last_rows
        which = pl.ds(0, 4) if part is None else pl.ds(2 * part, 2)
        if p == 0:
            return right_all.at[row, :, which, rows]
        return right_all.at[row, z, which, rows]

    def by_z(p, i, part=None):
        if p == 0:
            which = pl.ds(0, 4) if part is None else pl.ds(2 * part, 2)
            return right_all.at[near, z_at[i % 4], which, first_rows]
        which = pl.ds(0, 2) if part is None else part
        return right_all.at[which, z_at[i % 4], :, last_rows]

    def x_begin(p, sem):
        @pl.when(passing)
        def _():
            send(by_x(p, near), by_x(p, near), right_send, right_recv.at[sem], to_same)
            send(by_x(p, near), by_x(p, near), right_send, right_recv.at[sem], to_other)

    def x_forward(p, sem):
        drain(by_x(p, 0), right_recv.at[sem])

        @pl.when(passing)
        def _():
            send(by_x(p, 1 - near, 0), by_x(p, 1 - near, 0), right_send, right_recv.at[sem + 1], to_other)

        @pl.when(jnp.logical_not(passing))
        def _():
            send(by_x(p, 1 - near, 1), by_x(p, 1 - near, 1), right_send, right_recv.at[sem + 2], to_same)

    def x_end(p, sem):
        @pl.when(jnp.logical_not(passing))
        def _():
            drain(by_x(p, 0, 0), right_recv.at[sem + 1])
            drain(by_x(p, 0, 0), right_recv.at[sem + 2])

    def z_begin(p, sem):
        for k, sign in steps:
            send(by_z(p, 0), by_z(p, 0), right_send, right_recv.at[sem + k], along_z(sign))

    def z_forward(p, sem):
        for k, sign in steps:
            drain(by_z(p, 0), right_recv.at[sem + k])
            send(by_z(p, -sign, k), by_z(p, -sign, k), right_send, right_recv.at[sem + 2 + k], along_z(sign))

    def z_end(p, sem):
        for k in range(2):
            drain(by_z(p, 0, 0), right_recv.at[sem + 2 + k])

    @pl.when(passing)
    def _():
        drain(right_all.at[near, z], right_recv.at[0])
        z_begin(0, 1)
    x_begin(1, 5)

    @pl.when(passing)
    def _():
        z_forward(0, 1)
    x_forward(1, 5)

    @pl.when(passing)
    def _():
        z_end(0, 1)
    x_begin(0, 8)
    x_end(1, 5)
    z_begin(1, 11)
    x_forward(0, 8)
    z_forward(1, 11)
    x_end(0, 8)
    z_end(1, 11)
    drain(left_all, left_recv)

    def right_at(source, e2):
        return right_all[source // 16, (source // 4) % 4, source % 4, pl.ds(e2 * 8, 8), :]

    left_h, left_l = split(left_all[...])
    left_wide = jnp.concatenate([left_h, left_l, left_h], axis=-1)

    def sort(e2, carry):
        for t in range(16):
            first, second = merge_halves(
                right_at(2 * t, e2), right_at(2 * t + 1, e2))
            right_sorted[2 * e2, pl.ds(8 * t, 8), :] = first
            right_sorted[2 * e2 + 1, pl.ds(8 * t, 8), :] = second
        return carry

    lax.fori_loop(0, 16, sort, 0)

    def outer(e2, carry):
        high, low = split(right_sorted[pl.ds(2 * e2, 2)].reshape(256, 128))
        right_wide = jnp.concatenate([high, high, low], axis=-1)
        product = dot(left_wide, right_wide, NT)
        high, low = split(product)
        for i in range(16):
            for e1 in range(2):
                at = pl.ds(pl.multiple_of(64 * e2 + 32 * e1, 32), 32)
                lanes = slice(128 * (i % 2), 128 * (i % 2) + 128)
                rows, cols = slice(32 * i, 32 * i + 32), slice(128 * e1, 128 * e1 + 128)
                outer_h[i // 2, at, lanes] = high[rows, cols]
                outer_l[i // 2, at, lanes] = low[rows, cols]
        return carry

    lax.fori_loop(0, 16, outer, 0)

    def finish(i2, carry):
        out = dot3((couple_h[...], couple_l[...]), (outer_h[i2], outer_l[i2]))
        for i1 in range(2):
            out_ref[2 * i2 + i1] = jnp.transpose(out[:, 128 * i1:128 * i1 + 128])
        return carry

    lax.fori_loop(0, 8, finish, 0)

    for _ in range(31):
        drain(bias_ref, bias_send)
    drain(xs.at[0:31], x_send)
    drain(orr.at[0:127], o_send)
    drain(finals.at[0:192], final_send)
    drain(left_all.at[0:384], left_send)
    for y_to in range(2):
        @pl.when(jnp.logical_not((y == y_to) & (grp == pass_grp)))
        def _():
            drain(right_own, right_send)

    @pl.when(passing)
    def _():
        for _ in range(2):
            drain(by_z(0, 0), right_send)
            drain(by_z(0, 0, 0), right_send)
        for p in range(2):
            for _ in range(2):
                drain(by_x(p, 0), right_send)
    for p in range(2):
        drain(by_x(p, 0, 0), right_send)
    for _ in range(2):
        drain(by_z(1, 0), right_send)
        drain(by_z(1, 0, 0), right_send)


VM = pl.BlockSpec(memory_space=pltpu.VMEM)
SM = pl.BlockSpec(memory_space=pltpu.SMEM)
LIMIT = 58 * 1024 * 1024


def body(
    homolog_stack,
    couple_score_offset,
    strand_identity,
    strand_score_offset,
    homolog_presence,
    horizontal_matrix,
    horizontal_final_matrix,
    vertical_matrix,
    vertical_final_matrix,
    expand_matrix,
    shrink_matrix,
    tensor_matrix,
    couple_matrix,
):
    dma = pltpu.SemaphoreType.DMA
    regular = pltpu.SemaphoreType.REGULAR
    revised, pair = pl.pallas_call(
        kernel,
        out_shape=[
            jax.ShapeDtypeStruct((32, 2, 8, 256), F32),
            jax.ShapeDtypeStruct((16, 128, 128), F32),
        ],
        in_specs=[VM, VM, VM, SM] + [VM] * 9,
        out_specs=[VM, VM],
        scratch_shapes=[
            pltpu.VMEM((2, 4, 4, 2, 16, 512), F32),
            pltpu.VMEM((32, 2, 8, 256), F32),
            pltpu.VMEM((2, 32, 8, 256), F32),
            pltpu.VMEM((64, 2, 8, 128), F32),
            pltpu.VMEM((128, 8, 128), F32),
            pltpu.VMEM((256, 256), F32),
            pltpu.VMEM((256, 768), BF16),
            pltpu.VMEM((256, 768), BF16),
            pltpu.VMEM((4, 2, 32, 16, 256), BF16),
            pltpu.VMEM((4, 512, 256), BF16),
            pltpu.VMEM((4, 1024, 256), BF16),
            pltpu.VMEM((4, 32, 16, 128), F32),
            pltpu.VMEM((32, 16, 128), F32),
            pltpu.VMEM((2, 128, 512), F32),
            pltpu.VMEM((512, 256), F32),
            pltpu.VMEM((8, 512, 128), F32),
            pltpu.VMEM((2, 512, 128), F32),
            pltpu.VMEM((2, 512, 128), F32),
            pltpu.VMEM((128, 128), F32),
            pltpu.VMEM((128, 128), F32),
            pltpu.VMEM((512, 128), F32),
            pltpu.VMEM((2, 4, 4, 128, 128), F32),
            pltpu.VMEM((32, 128, 128), F32),
            pltpu.VMEM((8, 1024, 256), BF16),
            pltpu.VMEM((8, 1024, 256), BF16),
            pltpu.VMEM((128, 1024), BF16),
            pltpu.VMEM((128, 1024), BF16),
            dma, dma((22,)), dma, dma, dma, dma, dma, dma,
            dma, dma, dma, dma((15,)), regular, regular, regular,
        ],
        compiler_params=pltpu.CompilerParams(
            collective_id=0, has_side_effects=True, vmem_limit_bytes=LIMIT
        ),
        name="msa_block",
    )(
        homolog_stack.reshape(4, 32, 2, 8, 256),
        couple_score_offset,
        strand_identity.reshape(1, 512),
        strand_score_offset,
        jnp.swapaxes(horizontal_matrix, 1, 2),
        horizontal_final_matrix,
        homolog_presence.reshape(1, 128),
        vertical_matrix,
        vertical_final_matrix,
        expand_matrix,
        shrink_matrix,
        jnp.swapaxes(tensor_matrix, 1, 2),
        couple_matrix,
    )
    return revised.reshape(128, 4, 256), pair


def solution(mesh):
    return jax.shard_map(
        body,
        mesh=mesh,
        in_specs=(
            P("dap", None, None),
            P("grp", "dap", None),
            P(),
            P("grp"),
            P(),
            P(None, None, "grp"),
            P("grp", None),
            P(),
            P(),
            P(),
            P(),
            P(),
            P(),
        ),
        out_specs=(P(None, ("dap", "grp"), None), P("dap", "grp", None)),
        check_vma=False,
    )
```

time: 160 us -> 104 us (0.65)
  the two profiles are of different devices: /device:TPU:1 before, /device:TPU:8 now
where the time goes in v2:
time: 104 us
  Pallas kernels  98.8 us (95%)
  local copies, waits for them, and re-layouts  4.28 us (4%)
    pallas_call x1, Pallas kernels, body(): pl.pallas_call(kernel, out_shape=[jax.ShapeDtypeStruct((32, 2, 8, 256), F...  98.8 us
    unnamed x1, local copies, waits for them, and re-layouts  2.29 us

profile of v2, /device:TPU:8, one launch (start us, length us, event | category | flops | bytes accessed | tf_op | source)
XLA Modules:
  0.0 103.7 jit_solution(8538580282864738938)
XLA Ops:
  0.6 98.8 %msa_block.1 = (f32[32,2,8,256]{3,2,1,0:T(8,128)}, f32[16,128,128]{2,1,0:T(8,128)}) custom-call(f32[4,32,2,8,256]{4,3,2,1,0:T(8,128)} %bitcast.7, f32[2,16,512]{2,1,0:T(8,128)} %bias_ref.1, s32[1,512]{1,0:T(1,128)} %bitcast.10, f32[2]{0:T(128)} %offset_ref.1, f32[4,64,256]{2,1,0:T(8,128)} %bitcast.8, f32[64,256]{1,0:T(8,128)} %final_in_ref.1, ...), custom_call_target="tpu_custom_call" | custom-call | tf_op jit(solution)/shard_map/msa_block/pallas_call | solution.py:561
  99.5 2.0 %reshape.19 = f32[128,4,256]{2,1,0:T(4,128)} reshape(f32[32,2,8,256]{3,2,1,0:T(8,128)} %get-tuple-element.4) | data formatting | bytes 1048576 | tf_op jit(solution)/shard_map/reshape | solution.py:619
  101.4 2.3 %copy.16 = f32[16,128,128]{2,1,0:T(8,128)} copy(f32[16,128,128]{2,1,0:T(8,128)} %get-tuple-element.9) | data formatting | bytes 2097152

commit v3 on v2

v3 whole, which is shorter than its diff:
```python
import functools
import math

import jax
import jax.numpy as jnp
from jax import lax
from jax.experimental import pallas as pl
from jax.experimental.pallas import tpu as pltpu
from jax.sharding import PartitionSpec as P

F32 = jnp.float32
BF16 = jnp.bfloat16
MESH = pl.DeviceIdType.MESH
HEAD = 32
LOG2E = math.log2(math.e)
NN = (((1,), (0,)), ((), ()))
NT = (((1,), (1,)), ((), ()))


def split(a):
    high = a.astype(BF16)
    return high, (a - high.astype(F32)).astype(BF16)


def dot(a, b, dims=NN):
    return lax.dot_general(a, b, dims, preferred_element_type=F32)


def dot3(a, b, dims=NN):
    return dot(a[0], b[0], dims) + (dot(a[0], b[1], dims) + dot(a[1], b[0], dims))


def normed(rows):
    center = rows - jnp.mean(rows, axis=-1, keepdims=True)
    spread = jnp.mean(center * center, axis=-1, keepdims=True)
    return center * lax.rsqrt(spread + 1e-05)


def merge_halves(a, b):
    upper = lax.broadcasted_iota(jnp.int32, a.shape, a.ndim - 2) < 4
    first = jnp.where(upper, a, pltpu.roll(b, 4, axis=b.ndim - 2))
    second = jnp.where(upper, pltpu.roll(a, 4, axis=a.ndim - 2), b)
    return first, second


def lane_iota(shape):
    return lax.broadcasted_iota(jnp.int32, shape, len(shape) - 1)


def drain(ref, sem):
    pltpu.make_async_copy(ref, ref, sem).wait()


def signal(sem, device):
    pl.semaphore_signal(sem, inc=1, device_id=device, device_id_type=MESH)


def send(src, dst, send_sem, recv_sem, device):
    pltpu.make_async_remote_copy(
        src_ref=src, dst_ref=dst, send_sem=send_sem, recv_sem=recv_sem,
        device_id=device, device_id_type=MESH,
    ).start()


def kernel(
    x_ref, bias_ref, ids_ref, offset_ref, weight_ref, final_in_ref, live_ref, tensor_ref,
    vertical_in, final_in, expand_in, shrink_in, couple_in,
    revised_ref, out_ref,
    bias_all, xs, xr, os, og, finals, join_h, join_l, wide_h, wide_l, qs, ks, vs, gates, ids_col, chunk_bias,
    msa, proj, attended, units,
    left_own, right_own, left_all, right_all, outer_h, outer_l, couple_h, couple_l,
    vertical_h, vertical_l, last_h, last_l, expand_h, expand_l, shrink_h, shrink_l,
    bias_send, bias_recv, x_send, x_recv, o_send, o_recv, final_send, final_recv,
    left_send, left_recv, right_send, right_recv, near_z, near_x, near_y,
    vertical_ref, final_ref, expand_ref, shrink_ref, couple_ref, fetch,
):
    dap = lax.axis_index("dap")
    grp = lax.axis_index("grp")
    y, x, z = dap // 16, lax.rem(dap // 4, 4), lax.rem(dap, 4)
    x_at = [lax.rem(x + i, 4) for i in range(4)]
    z_at = [lax.rem(z + i, 4) for i in range(4)]

    def along_x(i):
        return y * 16 + x_at[i % 4] * 4 + z, grp

    def along_z(i):
        return y * 16 + x * 4 + z_at[i % 4], grp

    across_y = ((1 - y) * 16 + x * 4 + z, grp)

    barrier = pltpu.get_barrier_semaphore()
    for i in range(1, 4):
        signal(barrier, along_x(i))
        signal(barrier, along_z(i))
        signal(barrier, (dap, lax.rem(grp + i, 4)))
    signal(barrier, across_y)

    late = (
        (vertical_in, vertical_ref), (final_in, final_ref), (expand_in, expand_ref),
        (shrink_in, shrink_ref), (couple_in, couple_ref),
    )
    for i, (src, dst) in enumerate(late):
        pltpu.make_async_copy(src, dst, fetch.at[i]).start()

    zero = jnp.zeros((64, 256), F32)
    q_w = weight_ref[0] * (LOG2E / math.sqrt(HEAD))
    k_w, v_w, g_w = weight_ref[1], weight_ref[2], weight_ref[3]
    for at, parts in ((0, (q_w, q_w, q_w, zero)), (256, (k_w, k_w, k_w, zero)), (512, (v_w, v_w, g_w, g_w))):
        high, low = split(jnp.transpose(jnp.concatenate(parts, axis=0)))
        wide_h[:, at:at + 256] = high
        wide_l[:, at:at + 256] = low
    pl.semaphore_wait(barrier, 10)

    def unit(p, i, j, h=None):
        a, b = (x_at[j % 4], z_at[i % 4]) if p == 0 else (x_at[i % 4], z_at[j % 4])
        return bias_all.at[p, a, b] if h is None else bias_all.at[p, a, b, h]

    def line(p, j, h):
        return bias_all.at[0, x_at[j % 4], :, h] if p == 0 else bias_all.at[1, :, z_at[j % 4], h]

    def first_axis(p, i):
        return along_z(i) if p == 0 else along_x(i)

    def second_axis(p, i):
        return along_x(i) if p == 0 else along_z(i)

    steps = ((0, 1), (1, -1))
    own = bias_all.at[y, x, z]
    send(bias_ref, own, bias_send, bias_recv.at[0], across_y)
    pltpu.make_async_copy(bias_ref, own, bias_recv.at[21]).start()
    for i in range(1, 4):
        signal(near_z, along_z(i))
    drain(bias_ref, bias_recv.at[21])

    def own_path(act):
        for p in range(2):
            @pl.when(y == p)
            def _():
                act(p)

    def other_path(act):
        for p in range(2):
            @pl.when(y == 1 - p)
            def _():
                act(p)

    def spread(p):
        for i in (1, 3, 2):
            send(unit(p, 0, 0), unit(p, 0, 0), bias_send, bias_recv.at[1 + 10 * p], first_axis(p, i))

    def spread_line(p):
        drain(bias_all.at[0, 0, 0:3], bias_recv.at[1 + 10 * p])
        for k, sign in steps:
            send(line(p, 0, k), line(p, 0, k), bias_send, bias_recv.at[5 + 10 * p + k], second_axis(p, sign))
        for k, sign in steps:
            send(line(p, 0, 1 - k), line(p, 0, 1 - k), bias_send,
                 bias_recv.at[7 + 10 * p + k], second_axis(p, sign))

    def forward_line(p):
        for k, sign in steps:
            drain(line(0, 0, 0), bias_recv.at[5 + 10 * p + k])
            send(line(p, -sign, k), line(p, -sign, k), bias_send,
                 bias_recv.at[9 + 10 * p + k], second_axis(p, sign))

    own_path(spread)

    final_to = finals.at[pl.ds(pl.multiple_of(grp * 64, 64), 64)]
    pltpu.make_async_copy(final_in_ref, final_to, final_recv).start()
    for k in range(1, 4):
        send(final_in_ref, final_to, final_send, final_recv, (dap, lax.rem(grp + k, 4)))

    def project(s):
        rows = split(normed(x_ref[s].reshape(512, 256)))
        out = dot3(rows, (wide_h[...], wide_l[...]))
        lane = lane_iota((512, 256))
        head = lax.rem(lane, 64) // HEAD
        q_hi, q_lo = split(out[:, 0:256])
        q = jnp.where((lane >= 64) & (lane < 128), q_lo.astype(F32), q_hi.astype(F32))
        k_hi, k_lo = split(out[:, 256:512])
        k = jnp.where((lane >= 128) & (lane < 192), k_lo.astype(F32), k_hi.astype(F32))
        ks[s] = k.astype(BF16)
        lane_v = lane_iota((512, 128))
        head_v = lax.rem(lane_v, 64) // HEAD
        v_hi, v_lo = split(out[:, 512:640])
        v = jnp.where(lane_v >= 64, v_lo.astype(F32), v_hi.astype(F32))
        for h in range(2):
            qs[s, h] = jnp.where(head == h, q, 0.0).astype(BF16).reshape(32, 16, 256)
            vs[s, pl.ds(512 * h, 512), 0:128] = jnp.where(head_v == h, v, 0.0).astype(BF16)
            vs[s, pl.ds(512 * h, 512), 128:256] = jnp.where(head_v == h, 1.0, 0.0).astype(BF16)
        gates[s] = jax.nn.sigmoid(out[:, 640:768]).reshape(32, 16, 128)

    def project_and(s, carry):
        project(s)

        @pl.when(s == 0)
        def _():
            pl.semaphore_wait(near_z, 3)
            for i in range(1, 4):
                signal(near_x, along_x(i))
            drain(bias_ref, bias_recv.at[0])
            other_path(spread)

        @pl.when(s == 1)
        def _():
            own_path(spread_line)
            pl.semaphore_wait(near_x, 3)
            signal(near_y, across_y)

        @pl.when(s == 2)
        def _():
            other_path(spread_line)

        return carry

    lax.fori_loop(0, 4, project_and, 0)

    half = lax.rem(grp, 2)
    for s2 in range(2):
        first, second = merge_halves(x_ref[2 * s2, :, grp // 2], x_ref[2 * s2 + 1, :, grp // 2])
        xs[:, s2] = jnp.where(half == 0, first, second)
    for i in range(4):
        block = jnp.broadcast_to(ids_ref[:, 128 * i:128 * i + 128].astype(F32), (128, 128))
        ids_col[8 * i:8 * i + 8] = jnp.transpose(block).reshape(8, 16, 128)
    pl.semaphore_wait(near_y, 1)

    drain(finals, final_recv)
    gap = jnp.zeros((64, 256), F32)
    for s2 in range(2):
        pieces = []
        for g in range(4):
            piece = finals[64 * g:64 * g + 64, :]
            pieces += [piece, gap] if s2 == 0 else [gap, piece]
        join_h[s2], join_l[s2] = split(jnp.concatenate(pieces, axis=0))

    for i, (src, dst) in enumerate(late):
        pltpu.make_async_copy(src, dst, fetch.at[i]).wait()

    for m in range(4):
        w = vertical_ref[m]
        if m == 0:
            w = w * (LOG2E / math.sqrt(HEAD))
        vertical_h[m], vertical_l[m] = split(w)
    last_h[...], last_l[...] = split(final_ref[...])
    expand_h[...], expand_l[...] = split(expand_ref[...])
    shrink_h[...], shrink_l[...] = split(shrink_ref[...])
    for odd in range(2):
        for b in range(4):
            rows = jnp.concatenate(
                [couple_ref[pl.ds(2 * (4 * b + i) + odd, 32, stride=32), :] for i in range(4)], axis=0)
            at = 512 * odd + 128 * b
            couple_h[:, at:at + 128], couple_l[:, at:at + 128] = split(jnp.transpose(rows))

    def turned(step):
        turn = step + step // 2 - 2 * (step // 3)
        return lax.rem(x + turn, 4), lax.rem(z + turn, 4)

    def settle(step):
        x_now, z_now = turned(step)
        drain(og.at[:, 0, 0:2], o_recv.at[step])
        rows = split(jnp.concatenate(
            [jnp.concatenate([og[g, 0, x_now].reshape(32, 128), og[g, 1, :, z_now].reshape(32, 128)], axis=0)
             for g in range(4)], axis=-1))
        for s2 in range(2):
            out = dot3(rows, (join_h[s2], join_l[s2])).reshape(8, 8, 256)
            for i in range(4):
                xs[4 * x_now + i, s2] += out[i]
                xs[16 + 4 * i + z_now, s2] += out[4 + i]

        def send_x(k, carry):
            low_half = 1 - k // 4
            place = lax.rem(k + x + z, 4)
            to = low_half * (4 * x_now + place) + (1 - low_half) * (16 + 4 * place + z_now)

            @pl.when(to == dap)
            def _():
                pltpu.make_async_copy(xs.at[to], xr.at[:, dap], x_recv).start()

            @pl.when(to != dap)
            def _():
                send(xs.at[to], xr.at[:, dap], x_send, x_recv, (to, grp))

            return carry

        lax.fori_loop(0, 8, send_x, 0)

    def attend(step, carry):
        x_now, z_now = turned(step)

        @pl.when(step == 1)
        def _():
            own_path(forward_line)
            other_path(forward_line)
            for p in range(2):
                drain(line(0, 0, 0), bias_recv.at[7 + 10 * p + 1])

        @pl.when(step == 2)
        def _():
            for p in range(2):
                drain(line(0, 0, 0), bias_recv.at[7 + 10 * p])

        @pl.when(step == 3)
        def _():
            for p in range(2):
                for k in range(2):
                    drain(line(0, 0, 0), bias_recv.at[9 + 10 * p + k])

        def rows_of(ref, *lead):
            shape = ref.shape[-2:]
            upper = ref[(*lead, pl.ds(4 * x_now, 4))].reshape(64, shape[-1])
            return jnp.concatenate([upper] + [ref[(*lead, 16 + 4 * i + z_now)] for i in range(4)], axis=0)

        own_ids = rows_of(ids_col)
        same = (jnp.concatenate([own_ids] * 4, axis=-1) == ids_ref[...].astype(F32)).astype(F32)
        for h in range(2):
            here = jnp.concatenate(
                [bias_all[0, x_now, :, h].reshape(64, 512), bias_all[1, :, z_now, h].reshape(64, 512)], axis=0)
            chunk_bias[h] = (here + offset_ref[h] * same) * LOG2E
        outs = []
        for s in range(4):
            highs, lows = [], []
            for h in range(2):
                logits = dot(rows_of(qs, s, h), ks[s], NT) + chunk_bias[h]
                weights = jnp.exp2(logits - jnp.max(logits, axis=-1, keepdims=True))
                high, low = split(weights)
                highs.append(high)
                lows.append(low)
            v = vs[s]
            total = dot(jnp.concatenate(highs, axis=-1), v) + dot(jnp.concatenate(lows, axis=-1), v)
            top = total[:, 0:128]
            top = top + pltpu.roll(top, 64, axis=1)
            outs.append(top / total[:, 128:256] * rows_of(gates, s))
        left_lanes = lane_iota((128, 128)) < 64
        pair = [jnp.where(left_lanes, outs[s1], outs[2 + s1]).reshape(16, 8, 128) for s1 in range(2)]
        for side, tiles in enumerate(merge_halves(*pair)):
            tiles = tiles.reshape(8, 2, 8, 128)
            for t in range(2):
                os[2 * t + side, 0, x_now] = tiles[0:4, t]
                for i in range(4):
                    os[2 * t + side, 1, i, z_now] = tiles[4 + i, t]
        pltpu.make_async_copy(os.at[grp, 0, x_now], og.at[grp, 0, x_now], o_recv.at[step]).start()
        pltpu.make_async_copy(os.at[grp, 1, :, z_now], og.at[grp, 1, :, z_now], o_recv.at[step]).start()
        for k in (2, 1, 3):
            to = lax.rem(grp + k, 4)
            send(os.at[to, 0, x_now], og.at[grp, 0, x_now], o_send, o_recv.at[step], (dap, to))
            send(os.at[to, 1, :, z_now], og.at[grp, 1, :, z_now], o_send, o_recv.at[step], (dap, to))

        @pl.when(step > 0)
        def _():
            settle(step - 1)

        return carry

    lax.fori_loop(0, 4, attend, 0)
    settle(3)

    drain(xr, x_recv)

    for s2 in range(2):
        stack = xr[s2].reshape(256, 256)
        for part in range(2):
            msa[part, pl.ds(256 * s2, 256), :] = stack[:, 128 * part:128 * part + 128]

    rows = split(normed(jnp.concatenate([msa[0], msa[1]], axis=-1)))
    for m in range(4):
        out = dot3(rows, (vertical_h[m], vertical_l[m]))
        for part in range(2):
            proj[2 * m + part] = out[:, 128 * part:128 * part + 128]

    at = lax.broadcasted_iota(jnp.int32, (128, 128), 0)
    to = lax.broadcasted_iota(jnp.int32, (128, 128), 1)
    order = (at == 4 * lax.rem(to // 2, 32) + 2 * (to // 64) + lax.rem(to, 2)).astype(BF16)
    live = dot(live_ref[...].astype(F32).astype(BF16), order)
    live_total = jnp.sum(live)
    mask = (live - 1.0) * (1e9 * LOG2E)

    lane = lane_iota((128, 128))
    def attend_column(r):
        for part in range(2):
            q, k, v, g = (proj[2 * m + part, pl.ds(r, 128, stride=4), :] for m in range(4))
            q_h, q_l = split(q)
            k_h, k_l = split(k)
            v_h, v_l = split(v)
            keys = jnp.concatenate([k_h, k_h, k_l], axis=-1)
            wide_q, wide_v = [], []
            for h in range(4):
                mine = lane // HEAD == h
                none = jnp.zeros((128, 128), BF16)
                qm_h, qm_l = jnp.where(mine, q_h, none), jnp.where(mine, q_l, none)
                wide_q.append(jnp.concatenate([qm_h, qm_l, qm_h], axis=-1))
                wide_v.append(jnp.concatenate(
                    [jnp.where(mine, v_h, none), jnp.where(mine, v_l, none), mine.astype(BF16)], axis=-1))
            logits = dot(jnp.concatenate(wide_q, axis=0), keys, NT) + mask
            weights = jnp.exp2(logits - jnp.max(logits, axis=-1, keepdims=True))
            high, low = split(weights)
            values = jnp.concatenate(wide_v, axis=0)

            def heads_in_lanes(a):
                return jnp.concatenate([a[128 * h:128 * h + 128] for h in range(4)], axis=-1)

            total = dot(heads_in_lanes(high), values) + dot(heads_in_lanes(low), values)
            out = (total[:, 0:128] + total[:, 128:256]) / total[:, 256:384]
            attended[part, pl.ds(128 * (r % 2), 128), :] = out * jax.nn.sigmoid(g)

    narrow = split(tensor_ref[...].reshape(64, 256))

    def finish_column(turn):
        here = [pl.ds(2 * turn + r2, 128, stride=4) for r2 in range(2)]
        before = jnp.concatenate(
            [jnp.concatenate([msa[part, rows, :] for rows in here], axis=0) for part in range(2)], axis=-1)
        gated = split(jnp.concatenate([attended[0], attended[1]], axis=-1))
        current = before + dot3(gated, (last_h[...], last_l[...]))
        hidden = jnp.maximum(dot3(split(normed(current)), (expand_h[...], expand_l[...])), 0.0)
        revised = current + dot3(split(hidden), (shrink_h[...], shrink_l[...]))
        unit_high, unit_low = split(normed(revised))
        for r2 in range(2):
            mine = slice(128 * r2, 128 * r2 + 128)
            for part in range(2):
                units[part, here[r2], :] = revised[mine, 128 * part:128 * part + 128]
            both = dot3(narrow, (unit_high[mine], unit_low[mine]), NT)
            left_own[pl.ds(64 * turn + 32 * r2, 32), :] = both[0:32] * (live / live_total)
            right_own[turn, pl.ds(32 * r2, 32), :] = both[32:64] * live

    pass_grp = 2 * y + x // 2
    near = lax.rem(x, 2)
    passing = lax.rem(grp, 2) == x // 2
    to_same = (y * 16 + lax.rem(x + 1 + 2 * near, 4) * 4 + z, grp)
    to_other = (y * 16 + lax.rem(x + 3 + 2 * near, 4) * 4 + z, grp)
    top, low = pl.ds(0, 32), pl.ds(32, 32)

    def right_begin(turn):
        slot = right_all.at[turn, near, z, grp]
        for y_to in range(2):
            mine = (y == y_to) & (grp == pass_grp)

            @pl.when(mine)
            def _():
                pltpu.make_async_copy(right_own.at[turn], slot, right_recv.at[turn, 0]).start()

            @pl.when(jnp.logical_not(mine))
            def _():
                send(right_own.at[turn], slot, right_send, right_recv.at[turn, 0],
                     (y_to * 16 + x * 4 + z, pass_grp))

    def right_first(turn):
        @pl.when(passing)
        def _():
            drain(right_all.at[turn, near, z], right_recv.at[turn, 0])
            along = right_all.at[turn, near, z, :, top]
            for i in (1, 3, 2):
                send(along, along, right_send, right_recv.at[turn, 1], along_z(i))
            along = right_all.at[turn, near, z, :, low]
            for to in (to_same, to_other, along_x(2)):
                send(along, along, right_send, right_recv.at[turn, 2], to)

    def x_column(turn, row, part=None):
        which = pl.ds(0, 4) if part is None else pl.ds(2 * part, 2)
        return right_all.at[turn, row, :, which, top]

    def z_column(turn, i, part=None):
        which = pl.ds(0, 2) if part is None else part
        return right_all.at[turn, which, z_at[i % 4], :, low]

    def right_second(turn):
        @pl.when(passing)
        def _():
            drain(right_all.at[turn, near, 0:3, :, top], right_recv.at[turn, 1])
            for to in (to_same, to_other):
                send(x_column(turn, near), x_column(turn, near), right_send, right_recv.at[turn, 3], to)
            drain(right_all.at[turn, 0, z, :, low], right_recv.at[turn, 2])

        @pl.when(jnp.logical_not(passing))
        def _():
            drain(right_all.at[turn, :, z, :, low], right_recv.at[turn, 2])

        for k, sign in steps:
            send(z_column(turn, 0), z_column(turn, 0), right_send, right_recv.at[turn, 6 + k], along_z(sign))

    def right_third(turn):
        drain(x_column(turn, 0), right_recv.at[turn, 3])

        @pl.when(passing)
        def _():
            piece = x_column(turn, 1 - near, 0)
            send(piece, piece, right_send, right_recv.at[turn, 4], to_other)

        @pl.when(jnp.logical_not(passing))
        def _():
            piece = x_column(turn, 1 - near, 1)
            send(piece, piece, right_send, right_recv.at[turn, 5], to_same)

        for k, sign in steps:
            drain(z_column(turn, 0), right_recv.at[turn, 6 + k])
            piece = z_column(turn, -sign, k)
            send(piece, piece, right_send, right_recv.at[turn, 8 + k], along_z(sign))

    def right_end(turn):
        @pl.when(jnp.logical_not(passing))
        def _():
            for k in range(2):
                drain(x_column(turn, 0, 0), right_recv.at[turn, 4 + k])
        for k in range(2):
            drain(z_column(turn, 0, 0), right_recv.at[turn, 8 + k])

    def right_sent(turn):
        for y_to in range(2):
            @pl.when(jnp.logical_not((y == y_to) & (grp == pass_grp)))
            def _():
                drain(right_own.at[turn], right_send)

        @pl.when(passing)
        def _():
            for _ in range(2):
                drain(right_all.at[turn, 0, 0:3, :, top], right_send)
                drain(x_column(turn, 0), right_send)

        drain(x_column(turn, 0, 0), right_send)
        for k in range(2):
            drain(z_column(turn, 0), right_send)
            drain(z_column(turn, 0, 0), right_send)

    lane_low = lane_iota((256, 128)) < 64

    def outer(turn):
        left_h, left_l = split(left_all[...].reshape(8, 2, 32, 128))
        left_wide = [
            jnp.concatenate([a[:, odd].reshape(256, 128) for a in (left_h, left_l, left_h)], axis=-1)
            for odd in range(2)
        ]
        right_flat = right_all.reshape(2 * 32 * 64, 128)

        def step(quad, carry):
            wide = []
            for e in range(4):
                high, low = split(jnp.concatenate(
                    [right_flat[pl.ds(2048 * turn + 32 * r2 + 4 * quad + e, 32, stride=64), :] for r2 in range(2)],
                    axis=0))
                wide.append(jnp.concatenate([high, high, low], axis=-1))
            even = dot(left_wide[0], jnp.concatenate(wide, axis=0), NT)
            odd = dot(left_wide[1], jnp.concatenate([wide[1], wide[0], wide[3], wide[2]], axis=0), NT)
            for m in range(2):
                lanes = slice(128 * m, 128 * m + 128)
                a, b = even[:, lanes], odd[:, lanes]
                for side, mixed in enumerate((jnp.where(lane_low, a, b), jnp.where(lane_low, b, a))):
                    high, low = split(mixed)
                    at = pl.ds(pl.multiple_of(512 * side + 64 * quad + 32 * m, 32), 32)
                    for i in range(8):
                        cols = slice(128 * (i % 2), 128 * (i % 2) + 128)
                        outer_h[i // 2, at, cols] = high[32 * i:32 * i + 32]
                        outer_l[i // 2, at, cols] = low[32 * i:32 * i + 32]
            return carry

        lax.fori_loop(0, 8, step, 0)

    def finish(turn):
        def step(i4, carry):
            total = []
            for side in range(2):
                at = slice(512 * side, 512 * side + 512)
                total.append(dot3((couple_h[:, at], couple_l[:, at]), (outer_h[i4, at, :], outer_l[i4, at, :])))
            for i2 in range(2):
                lanes = slice(128 * i2, 128 * i2 + 128)
                block = jnp.transpose(total[0][:, lanes] + pltpu.roll(total[1][:, lanes], 64, axis=1))
                for i1 in range(2):
                    for r2 in range(2):
                        at = 64 * i1 + 32 * r2
                        out_ref[4 * i4 + 2 * i2 + i1, pl.ds(2 * turn + r2, 32, stride=4), :] = block[at:at + 32]
            return carry

        lax.fori_loop(0, 4, step, 0)

    attend_column(0)
    attend_column(1)
    finish_column(0)
    right_begin(0)
    attend_column(2)
    attend_column(3)
    right_first(0)
    finish_column(1)
    right_begin(1)
    right_second(0)
    right_first(1)
    left_to = left_all.at[pl.ds(pl.multiple_of(grp * 128, 128), 128)]
    pltpu.make_async_copy(left_own, left_to, left_recv).start()
    for k in range(1, 4):
        send(left_own, left_to, left_send, left_recv, (dap, lax.rem(grp + k, 4)))
    right_third(0)
    right_second(1)
    for s2 in range(2):
        for part in range(2):
            revised_ref[:, s2, :, 128 * part:128 * part + 128] = units[part, pl.ds(256 * s2, 256), :].reshape(32, 8, 128)
    right_end(0)
    drain(left_all, left_recv)
    outer(0)
    right_third(1)
    finish(0)
    right_end(1)
    outer(1)
    finish(1)

    for _ in range(31):
        drain(bias_ref, bias_send)
    drain(xs.at[0:31], x_send)
    drain(og.at[0:3], o_send)
    drain(finals.at[0:192], final_send)
    drain(left_all.at[0:384], left_send)
    for turn in range(2):
        right_sent(turn)


VM = pl.BlockSpec(memory_space=pltpu.VMEM)
SM = pl.BlockSpec(memory_space=pltpu.SMEM)
LIMIT = 58 * 1024 * 1024


def body(
    homolog_stack,
    couple_score_offset,
    strand_identity,
    strand_score_offset,
    homolog_presence,
    horizontal_matrix,
    horizontal_final_matrix,
    vertical_matrix,
    vertical_final_matrix,
    expand_matrix,
    shrink_matrix,
    tensor_matrix,
    couple_matrix,
):
    dma = pltpu.SemaphoreType.DMA
    regular = pltpu.SemaphoreType.REGULAR
    revised, pair = pl.pallas_call(
        kernel,
        out_shape=[
            jax.ShapeDtypeStruct((32, 2, 8, 256), F32),
            jax.ShapeDtypeStruct((16, 128, 128), F32),
        ],
        in_specs=[VM, VM, VM, SM] + [VM] * 4 + [pl.BlockSpec(memory_space=pl.ANY)] * 5,
        out_specs=[VM, VM],
        scratch_shapes=[
            pltpu.VMEM((2, 4, 4, 2, 16, 512), F32),
            pltpu.VMEM((32, 2, 8, 256), F32),
            pltpu.VMEM((2, 32, 8, 256), F32),
            pltpu.VMEM((4, 2, 4, 4, 8, 128), F32),
            pltpu.VMEM((4, 2, 4, 4, 8, 128), F32),
            pltpu.VMEM((256, 256), F32),
            pltpu.VMEM((2, 512, 256), BF16),
            pltpu.VMEM((2, 512, 256), BF16),
            pltpu.VMEM((256, 768), BF16),
            pltpu.VMEM((256, 768), BF16),
            pltpu.VMEM((4, 2, 32, 16, 256), BF16),
            pltpu.VMEM((4, 512, 256), BF16),
            pltpu.VMEM((4, 1024, 256), BF16),
            pltpu.VMEM((4, 32, 16, 128), F32),
            pltpu.VMEM((32, 16, 128), F32),
            pltpu.VMEM((2, 128, 512), F32),
            pltpu.VMEM((2, 512, 128), F32),
            pltpu.VMEM((8, 512, 128), F32),
            pltpu.VMEM((2, 256, 128), F32),
            pltpu.VMEM((2, 512, 128), F32),
            pltpu.VMEM((128, 128), F32),
            pltpu.VMEM((2, 64, 128), F32),
            pltpu.VMEM((512, 128), F32),
            pltpu.VMEM((2, 2, 4, 4, 64, 128), F32),
            pltpu.VMEM((4, 1024, 256), BF16),
            pltpu.VMEM((4, 1024, 256), BF16),
            pltpu.VMEM((128, 1024), BF16),
            pltpu.VMEM((128, 1024), BF16),
            pltpu.VMEM((4, 256, 256), BF16),
            pltpu.VMEM((4, 256, 256), BF16),
            pltpu.VMEM((256, 256), BF16),
            pltpu.VMEM((256, 256), BF16),
            pltpu.VMEM((256, 1024), BF16),
            pltpu.VMEM((256, 1024), BF16),
            pltpu.VMEM((1024, 256), BF16),
            pltpu.VMEM((1024, 256), BF16),
            dma, dma((22,)), dma, dma, dma, dma((4,)), dma, dma,
            dma, dma, dma, dma((2, 10)), regular, regular, regular,
            pltpu.VMEM((4, 256, 256), F32),
            pltpu.VMEM((256, 256), F32),
            pltpu.VMEM((256, 1024), F32),
            pltpu.VMEM((1024, 256), F32),
            pltpu.VMEM((1024, 128), F32),
            dma((5,)),
        ],
        compiler_params=pltpu.CompilerParams(
            collective_id=0, has_side_effects=True, vmem_limit_bytes=LIMIT
        ),
        name="msa_block",
    )(
        homolog_stack.reshape(4, 32, 2, 8, 256),
        couple_score_offset,
        strand_identity.reshape(1, 512),
        strand_score_offset,
        jnp.swapaxes(horizontal_matrix, 1, 2),
        horizontal_final_matrix,
        homolog_presence.reshape(1, 128),
        jnp.swapaxes(tensor_matrix, 1, 2),
        vertical_matrix,
        vertical_final_matrix,
        expand_matrix,
        shrink_matrix,
        couple_matrix,
    )
    return revised.reshape(128, 4, 256), pair


def solution(mesh):
    return jax.shard_map(
        body,
        mesh=mesh,
        in_specs=(
            P("dap", None, None),
            P("grp", "dap", None),
            P(),
            P("grp"),
            P(),
            P(None, None, "grp"),
            P("grp", None),
            P(),
            P(),
            P(),
            P(),
            P(),
            P(),
        ),
        out_specs=(P(None, ("dap", "grp"), None), P("dap", "grp", None)),
        check_vma=False,
    )
```

time: 104 us -> 89.6 us (0.86)
  the two profiles are of different devices: /device:TPU:8 before, /device:TPU:1 now
where the time goes in v3:
time: 89.6 us; the launch traced here: 88.3 us
  Pallas kernels  83.4 us (93%)
  local copies, waits for them, and re-layouts  4.28 us (5%)
    pallas_call x1, Pallas kernels, body(): pl.pallas_call(kernel, out_shape=[jax.ShapeDtypeStruct((32, 2, 8, 256), F...  83.4 us
    unnamed x1, local copies, waits for them, and re-layouts  2.29 us
    reshape x1, local copies, waits for them, and re-layouts, body(): return (revised.reshape(128, 4, 256), pair)  1.98 us

profile of v3, /device:TPU:1, one launch (start us, length us, event | category | flops | bytes accessed | tf_op | source)
XLA Modules:
  0.0 88.3 jit_solution(17947199746535114912)
XLA Ops:
  0.6 83.4 %msa_block.1 = (f32[32,2,8,256]{3,2,1,0:T(8,128)}, f32[16,128,128]{2,1,0:T(8,128)}) custom-call(f32[4,32,2,8,256]{4,3,2,1,0:T(8,128)} %bitcast.7, f32[2,16,512]{2,1,0:T(8,128)} %bias_ref.1, s32[1,512]{1,0:T(1,128)} %bitcast.10, f32[2]{0:T(128)} %offset_ref.1, f32[4,64,256]{2,1,0:T(8,128)} %bitcast.8, f32[64,256]{1,0:T(8,128)} %final_in_ref.1, ...), custom_call_target="tpu_custom_call" | custom-call | tf_op jit(solution)/shard_map/msa_block/pallas_call | solution.py:632
  84.0 2.0 %reshape.19 = f32[128,4,256]{2,1,0:T(4,128)} reshape(f32[32,2,8,256]{3,2,1,0:T(8,128)} %get-tuple-element.4) | data formatting | bytes 1048576 | tf_op jit(solution)/shard_map/reshape | solution.py:705
  86.0 2.3 %copy.16 = f32[16,128,128]{2,1,0:T(8,128)} copy(f32[16,128,128]{2,1,0:T(8,128)} %get-tuple-element.9) | data formatting | bytes 2097152

commit v4 on v3

--- a/solution.py
+++ b/solution.py
@@ -27,7 +27,9 @@
 
 
 def dot3(a, b, dims=NN):
-    return dot(a[0], b[0], dims) + (dot(a[0], b[1], dims) + dot(a[1], b[0], dims))
+    rows = a[0].shape[0]
+    both = dot(jnp.concatenate(a, axis=0), b[0], dims)
+    return both[:rows] + (both[rows:] + dot(a[0], b[1], dims))
 
 
 def normed(rows):
@@ -63,9 +65,9 @@
 
 
 def kernel(
-    x_ref, bias_ref, ids_ref, offset_ref, weight_ref, final_in_ref, live_ref, tensor_ref,
+    x_in, bias_ref, ids_ref, offset_ref, weight_ref, final_in_ref, live_ref, tensor_ref,
     vertical_in, final_in, expand_in, shrink_in, couple_in,
-    revised_ref, out_ref,
+    revised_hbm, out_hbm,
     bias_all, xs, xr, os, og, finals, join_h, join_l, wide_h, wide_l, qs, ks, vs, gates, ids_col, chunk_bias,
     msa, proj, attended, units,
     left_own, right_own, left_all, right_all, outer_h, outer_l, couple_h, couple_l,
@@ -73,6 +75,7 @@
     bias_send, bias_recv, x_send, x_recv, o_send, o_recv, final_send, final_recv,
     left_send, left_recv, right_send, right_recv, near_z, near_x, near_y,
     vertical_ref, final_ref, expand_ref, shrink_ref, couple_ref, fetch,
+    x_ref, x_fetch, revised_ref, out_ref, out_copy,
 ):
     dap = lax.axis_index("dap")
     grp = lax.axis_index("grp")
@@ -99,6 +102,8 @@
         (vertical_in, vertical_ref), (final_in, final_ref), (expand_in, expand_ref),
         (shrink_in, shrink_ref), (couple_in, couple_ref),
     )
+    for s in range(4):
+        pltpu.make_async_copy(x_in.at[s], x_ref.at[s], x_fetch.at[s]).start()
     for i, (src, dst) in enumerate(late):
         pltpu.make_async_copy(src, dst, fetch.at[i]).start()
 
@@ -170,6 +175,7 @@
         send(final_in_ref, final_to, final_send, final_recv, (dap, lax.rem(grp + k, 4)))
 
     def project(s):
+        pltpu.make_async_copy(x_in.at[s], x_ref.at[s], x_fetch.at[s]).wait()
         rows = split(normed(x_ref[s].reshape(512, 256)))
         out = dot3(rows, (wide_h[...], wide_l[...]))
         lane = lane_iota((512, 256))
@@ -318,14 +324,16 @@
         outs = []
         for s in range(4):
             highs, lows = [], []
+            both = dot(jnp.concatenate([rows_of(qs, s, h) for h in range(2)], axis=0), ks[s], NT)
             for h in range(2):
-                logits = dot(rows_of(qs, s, h), ks[s], NT) + chunk_bias[h]
+                logits = both[128 * h:128 * h + 128] + chunk_bias[h]
                 weights = jnp.exp2(logits - jnp.max(logits, axis=-1, keepdims=True))
                 high, low = split(weights)
                 highs.append(high)
                 lows.append(low)
             v = vs[s]
-            total = dot(jnp.concatenate(highs, axis=-1), v) + dot(jnp.concatenate(lows, axis=-1), v)
+            total = dot(jnp.concatenate([jnp.concatenate(a, axis=-1) for a in (highs, lows)], axis=0), v)
+            total = total[0:128] + total[128:256]
             top = total[:, 0:128]
             top = top + pltpu.roll(top, 64, axis=1)
             outs.append(top / total[:, 128:256] * rows_of(gates, s))
@@ -397,7 +405,8 @@
             def heads_in_lanes(a):
                 return jnp.concatenate([a[128 * h:128 * h + 128] for h in range(4)], axis=-1)
 
-            total = dot(heads_in_lanes(high), values) + dot(heads_in_lanes(low), values)
+            total = dot(jnp.concatenate([heads_in_lanes(high), heads_in_lanes(low)], axis=0), values)
+            total = total[0:128] + total[128:256]
             out = (total[:, 0:128] + total[:, 128:256]) / total[:, 256:384]
             attended[part, pl.ds(128 * (r % 2), 128), :] = out * jax.nn.sigmoid(g)
 
@@ -549,7 +558,7 @@
                         outer_l[i // 2, at, cols] = low[32 * i:32 * i + 32]
             return carry
 
-        lax.fori_loop(0, 8, step, 0)
+        lax.fori_loop(0, 8, step, 0, unroll=2)
 
     def finish(turn):
         def step(i4, carry):
@@ -564,9 +573,12 @@
                     for r2 in range(2):
                         at = 64 * i1 + 32 * r2
                         out_ref[4 * i4 + 2 * i2 + i1, pl.ds(2 * turn + r2, 32, stride=4), :] = block[at:at + 32]
+            if turn == 1:
+                four = pl.ds(4 * i4, 4)
+                pltpu.make_async_copy(out_ref.at[four], out_hbm.at[four], out_copy.at[i4]).start()
             return carry
 
-        lax.fori_loop(0, 4, step, 0)
+        lax.fori_loop(0, 4, step, 0, unroll=2)
 
     attend_column(0)
     attend_column(1)
@@ -587,7 +599,10 @@
     right_second(1)
     for s2 in range(2):
         for part in range(2):
-            revised_ref[:, s2, :, 128 * part:128 * part + 128] = units[part, pl.ds(256 * s2, 256), :].reshape(32, 8, 128)
+            tiles = units[part, pl.ds(256 * s2, 256), :].reshape(32, 8, 128)
+            for s1 in range(2):
+                revised_ref[:, s2, s1, :, 128 * part:128 * part + 128] = tiles[:, 4 * s1:4 * s1 + 4]
+    pltpu.make_async_copy(revised_ref, revised_hbm, out_copy.at[4]).start()
     right_end(0)
     drain(left_all, left_recv)
     outer(0)
@@ -597,6 +612,10 @@
     outer(1)
     finish(1)
 
+    for i in range(4):
+        four = pl.ds(4 * i, 4)
+        pltpu.make_async_copy(out_ref.at[four], out_hbm.at[four], out_copy.at[i]).wait()
+    pltpu.make_async_copy(revised_ref, revised_hbm, out_copy.at[4]).wait()
     for _ in range(31):
         drain(bias_ref, bias_send)
     drain(xs.at[0:31], x_send)
@@ -607,8 +626,23 @@
         right_sent(turn)
 
 
+def emit_kernel(revised_in, pair_in, revised_out, pair_out, revised, pair, sems):
+    copies = [(revised_in, revised, revised_out)]
+    for i in range(4):
+        four = pl.ds(4 * i, 4)
+        copies.append((pair_in.at[four], pair.at[four], pair_out.at[four]))
+    for i, (src, here, dst) in enumerate(copies):
+        pltpu.make_async_copy(src, here, sems.at[0, i]).start()
+    for i, (src, here, dst) in enumerate(copies):
+        pltpu.make_async_copy(src, here, sems.at[0, i]).wait()
+        pltpu.make_async_copy(here, dst, sems.at[1, i]).start()
+    for i, (src, here, dst) in enumerate(copies):
+        pltpu.make_async_copy(here, dst, sems.at[1, i]).wait()
+
+
 VM = pl.BlockSpec(memory_space=pltpu.VMEM)
 SM = pl.BlockSpec(memory_space=pltpu.SMEM)
+ANY = pl.BlockSpec(memory_space=pl.ANY)
 LIMIT = 58 * 1024 * 1024
 
 
@@ -632,11 +666,11 @@
     revised, pair = pl.pallas_call(
         kernel,
         out_shape=[
-            jax.ShapeDtypeStruct((32, 2, 8, 256), F32),
+            jax.ShapeDtypeStruct((32, 2, 2, 4, 256), F32),
             jax.ShapeDtypeStruct((16, 128, 128), F32),
         ],
-        in_specs=[VM, VM, VM, SM] + [VM] * 4 + [pl.BlockSpec(memory_space=pl.ANY)] * 5,
-        out_specs=[VM, VM],
+        in_specs=[ANY, VM, VM, SM] + [VM] * 4 + [ANY] * 5,
+        out_specs=[ANY, ANY],
         scratch_shapes=[
             pltpu.VMEM((2, 4, 4, 2, 16, 512), F32),
             pltpu.VMEM((32, 2, 8, 256), F32),
@@ -682,6 +716,11 @@
             pltpu.VMEM((1024, 256), F32),
             pltpu.VMEM((1024, 128), F32),
             dma((5,)),
+            pltpu.VMEM((4, 32, 2, 8, 256), F32),
+            dma((4,)),
+            pltpu.VMEM((32, 2, 2, 4, 256), F32),
+            pltpu.VMEM((16, 128, 128), F32),
+            dma((5,)),
         ],
         compiler_params=pltpu.CompilerParams(
             collective_id=0, has_side_effects=True, vmem_limit_bytes=LIMIT
@@ -702,6 +741,19 @@
         shrink_matrix,
         couple_matrix,
     )
+    revised, pair = pl.pallas_call(
+        emit_kernel,
+        out_shape=[
+            jax.ShapeDtypeStruct((32, 2, 2, 4, 256), F32),
+            jax.ShapeDtypeStruct((16, 128, 128), F32),
+        ],
+        in_specs=[ANY, ANY],
+        out_specs=[ANY, ANY],
+        scratch_shapes=[
+            pltpu.VMEM((32, 2, 2, 4, 256), F32), pltpu.VMEM((16, 128, 128), F32), dma((2, 5)),
+        ],
+        name="emit",
+    )(revised, pair)
     return revised.reshape(128, 4, 256), pair
 
 

time: 89.6 us -> 83.2 us (0.929); the launches traced: 88.3 us -> 83.1 us
  local copies, waits for them, and re-layouts: 4.28 us -> 0 us
  Pallas kernels: 83.4 us -> 82.3 us
    unnamed x1 -> x0, local copies, waits for them, and re-layouts: 2.29 us -> none
    reshape x1 -> x0, local copies, waits for them, and re-layouts: 1.98 us -> none  [body(): return (revised.reshape(128, 4, 256), pair)]
    pallas_call x1 -> x2, Pallas kernels: 83.4 us -> 82.3 us  [the longest x1 80 us: body(): pl.pallas_call(kernel, out_shape=[jax.ShapeDtypeStruct((32, 2, 2, 4, 256)...]
where the time goes in v4:
time: 83.2 us; the launch traced here: 83.1 us
  Pallas kernels  82.3 us (99%)
    pallas_call x1, Pallas kernels, body(): pl.pallas_call(kernel, out_shape=[jax.ShapeDtypeStruct((32, 2, 2, 4, 256)...  80 us
    pallas_call x1, Pallas kernels, body(): pl.pallas_call(emit_kernel, out_shape=[jax.ShapeDtypeStruct((32, 2, 2, 4,...  2.26 us

profile of v4, /device:TPU:1, one launch (start us, length us, event | category | flops | bytes accessed | tf_op | source)
XLA Modules:
  0.0 83.1 jit_solution(2384331448494950943)
XLA Ops:
  0.6 80.0 %msa_block.1 = (f32[32,2,2,4,256]{4,3,2,1,0:T(4,128)}, f32[16,128,128]{2,1,0:T(8,128)}) custom-call(f32[4,32,2,8,256]{4,3,2,1,0:T(8,128)} %bitcast.6, f32[2,16,512]{2,1,0:T(8,128)} %bias_ref.1, s32[1,512]{1,0:T(1,128)} %bitcast.9, f32[2]{0:T(128)} %offset_ref.1, f32[4,64,256]{2,1,0:T(8,128)} %bitcast.7, f32[64,256]{1,0:T(8,128)} %final_in_ref.1, ...), custom_call_target="tpu_custom_call" | custom-call | tf_op jit(solution)/shard_map/msa_block/pallas_call | solution.py:666
  80.6 2.3 %emit.1 = (f32[32,2,2,4,256]{4,3,2,1,0:T(4,128)}, f32[16,128,128]{2,1,0:T(8,128)}) custom-call(f32[32,2,2,4,256]{4,3,2,1,0:T(4,128)} %get-tuple-element.6.revised_in, f32[16,128,128]{2,1,0:T(8,128)} %get-tuple-element.7.pair_in), custom_call_target="tpu_custom_call" | custom-call | tf_op jit(solution)/shard_map/emit/pallas_call | solution.py:744

commit v5 on v4

--- a/solution.py
+++ b/solution.py
@@ -408,33 +408,29 @@
             total = dot(jnp.concatenate([heads_in_lanes(high), heads_in_lanes(low)], axis=0), values)
             total = total[0:128] + total[128:256]
             out = (total[:, 0:128] + total[:, 128:256]) / total[:, 256:384]
-            attended[part, pl.ds(128 * (r % 2), 128), :] = out * jax.nn.sigmoid(g)
+            attended[part] = out * jax.nn.sigmoid(g)
 
     narrow = split(tensor_ref[...].reshape(64, 256))
 
     def finish_column(turn):
-        here = [pl.ds(2 * turn + r2, 128, stride=4) for r2 in range(2)]
-        before = jnp.concatenate(
-            [jnp.concatenate([msa[part, rows, :] for rows in here], axis=0) for part in range(2)], axis=-1)
+        here = pl.ds(turn, 128, stride=4)
+        before = jnp.concatenate([msa[part, here, :] for part in range(2)], axis=-1)
         gated = split(jnp.concatenate([attended[0], attended[1]], axis=-1))
         current = before + dot3(gated, (last_h[...], last_l[...]))
         hidden = jnp.maximum(dot3(split(normed(current)), (expand_h[...], expand_l[...])), 0.0)
         revised = current + dot3(split(hidden), (shrink_h[...], shrink_l[...]))
-        unit_high, unit_low = split(normed(revised))
-        for r2 in range(2):
-            mine = slice(128 * r2, 128 * r2 + 128)
-            for part in range(2):
-                units[part, here[r2], :] = revised[mine, 128 * part:128 * part + 128]
-            both = dot3(narrow, (unit_high[mine], unit_low[mine]), NT)
-            left_own[pl.ds(64 * turn + 32 * r2, 32), :] = both[0:32] * (live / live_total)
-            right_own[turn, pl.ds(32 * r2, 32), :] = both[32:64] * live
+        for part in range(2):
+            units[part, here, :] = revised[:, 128 * part:128 * part + 128]
+        both = dot3(narrow, split(normed(revised)), NT)
+        left_own[pl.ds(32 * turn, 32), :] = both[0:32] * (live / live_total)
+        right_own[turn] = both[32:64] * live
 
     pass_grp = 2 * y + x // 2
     near = lax.rem(x, 2)
     passing = lax.rem(grp, 2) == x // 2
     to_same = (y * 16 + lax.rem(x + 1 + 2 * near, 4) * 4 + z, grp)
     to_other = (y * 16 + lax.rem(x + 3 + 2 * near, 4) * 4 + z, grp)
-    top, low = pl.ds(0, 32), pl.ds(32, 32)
+    top, low = pl.ds(0, 16), pl.ds(16, 16)
 
     def right_begin(turn):
         slot = right_all.at[turn, near, z, grp]
@@ -535,13 +531,13 @@
             jnp.concatenate([a[:, odd].reshape(256, 128) for a in (left_h, left_l, left_h)], axis=-1)
             for odd in range(2)
         ]
-        right_flat = right_all.reshape(2 * 32 * 64, 128)
+        right_flat = right_all.reshape(4 * 32 * 32, 128)
 
         def step(quad, carry):
             wide = []
             for e in range(4):
                 high, low = split(jnp.concatenate(
-                    [right_flat[pl.ds(2048 * turn + 32 * r2 + 4 * quad + e, 32, stride=64), :] for r2 in range(2)],
+                    [right_flat[pl.ds(1024 * (2 * turn + r2) + 4 * quad + e, 32, stride=32), :] for r2 in range(2)],
                     axis=0))
                 wide.append(jnp.concatenate([high, high, low], axis=-1))
             even = dot(left_wide[0], jnp.concatenate(wide, axis=0), NT)
@@ -558,7 +554,7 @@
                         outer_l[i // 2, at, cols] = low[32 * i:32 * i + 32]
             return carry
 
-        lax.fori_loop(0, 8, step, 0, unroll=2)
+        lax.fori_loop(0, 8, step, 0, unroll=4)
 
     def finish(turn):
         def step(i4, carry):
@@ -578,37 +574,49 @@
                 pltpu.make_async_copy(out_ref.at[four], out_hbm.at[four], out_copy.at[i4]).start()
             return carry
 
-        lax.fori_loop(0, 4, step, 0, unroll=2)
+        lax.fori_loop(0, 4, step, 0, unroll=4)
 
     attend_column(0)
-    attend_column(1)
     finish_column(0)
     right_begin(0)
-    attend_column(2)
-    attend_column(3)
-    right_first(0)
+    attend_column(1)
     finish_column(1)
     right_begin(1)
+    attend_column(2)
+    right_first(0)
+    finish_column(2)
+    right_begin(2)
+    attend_column(3)
+    right_first(1)
+    finish_column(3)
+    right_begin(3)
     right_second(0)
-    right_first(1)
+    right_first(2)
+    right_second(1)
+    right_first(3)
     left_to = left_all.at[pl.ds(pl.multiple_of(grp * 128, 128), 128)]
     pltpu.make_async_copy(left_own, left_to, left_recv).start()
     for k in range(1, 4):
         send(left_own, left_to, left_send, left_recv, (dap, lax.rem(grp + k, 4)))
+    right_second(2)
     right_third(0)
-    right_second(1)
+    right_second(3)
+    right_third(1)
     for s2 in range(2):
         for part in range(2):
             tiles = units[part, pl.ds(256 * s2, 256), :].reshape(32, 8, 128)
             for s1 in range(2):
                 revised_ref[:, s2, s1, :, 128 * part:128 * part + 128] = tiles[:, 4 * s1:4 * s1 + 4]
     pltpu.make_async_copy(revised_ref, revised_hbm, out_copy.at[4]).start()
+    right_third(2)
     right_end(0)
+    right_end(1)
     drain(left_all, left_recv)
+    right_third(3)
     outer(0)
-    right_third(1)
     finish(0)
-    right_end(1)
+    right_end(2)
+    right_end(3)
     outer(1)
     finish(1)
 
@@ -622,7 +630,7 @@
     drain(og.at[0:3], o_send)
     drain(finals.at[0:192], final_send)
     drain(left_all.at[0:384], left_send)
-    for turn in range(2):
+    for turn in range(4):
         right_sent(turn)
 
 
@@ -690,12 +698,12 @@
             pltpu.VMEM((2, 128, 512), F32),
             pltpu.VMEM((2, 512, 128), F32),
             pltpu.VMEM((8, 512, 128), F32),
-            pltpu.VMEM((2, 256, 128), F32),
+            pltpu.VMEM((2, 128, 128), F32),
             pltpu.VMEM((2, 512, 128), F32),
             pltpu.VMEM((128, 128), F32),
-            pltpu.VMEM((2, 64, 128), F32),
+            pltpu.VMEM((4, 32, 128), F32),
             pltpu.VMEM((512, 128), F32),
-            pltpu.VMEM((2, 2, 4, 4, 64, 128), F32),
+            pltpu.VMEM((4, 2, 4, 4, 32, 128), F32),
             pltpu.VMEM((4, 1024, 256), BF16),
             pltpu.VMEM((4, 1024, 256), BF16),
             pltpu.VMEM((128, 1024), BF16),
@@ -709,7 +717,7 @@
             pltpu.VMEM((1024, 256), BF16),
             pltpu.VMEM((1024, 256), BF16),
             dma, dma((22,)), dma, dma, dma, dma((4,)), dma, dma,
-            dma, dma, dma, dma((2, 10)), regular, regular, regular,
+            dma, dma, dma, dma((4, 10)), regular, regular, regular,
             pltpu.VMEM((4, 256, 256), F32),
             pltpu.VMEM((256, 256), F32),
             pltpu.VMEM((256, 1024), F32),

time: 83.2 us -> 80.7 us (0.970)
  Pallas kernels: 82.3 us -> 79.7 us
    pallas_call x1, Pallas kernels: 80 us -> 77.5 us  [body(): pl.pallas_call(kernel, out_shape=[jax.ShapeDtypeStruct((32, 2, 2, 4, 256)...]
where the time goes in v5:
time: 80.7 us; the launch traced here: 80.5 us
  Pallas kernels  79.7 us (99%)
    pallas_call x1, Pallas kernels, body(): pl.pallas_call(kernel, out_shape=[jax.ShapeDtypeStruct((32, 2, 2, 4, 256)...  77.5 us
    pallas_call x1, Pallas kernels, body(): pl.pallas_call(emit_kernel, out_shape=[jax.ShapeDtypeStruct((32, 2, 2, 4,...  2.26 us

profile of v5, /device:TPU:1, one launch (start us, length us, event | category | flops | bytes accessed | tf_op | source)
XLA Modules:
  0.0 80.5 jit_solution(5901808716357342426)
XLA Ops:
  0.6 77.5 %msa_block.1 = (f32[32,2,2,4,256]{4,3,2,1,0:T(4,128)}, f32[16,128,128]{2,1,0:T(8,128)}) custom-call(f32[4,32,2,8,256]{4,3,2,1,0:T(8,128)} %bitcast.6, f32[2,16,512]{2,1,0:T(8,128)} %bias_ref.1, s32[1,512]{1,0:T(1,128)} %bitcast.9, f32[2]{0:T(128)} %offset_ref.1, f32[4,64,256]{2,1,0:T(8,128)} %bitcast.7, f32[64,256]{1,0:T(8,128)} %final_in_ref.1, ...), custom_call_target="tpu_custom_call" | custom-call | tf_op jit(solution)/shard_map/msa_block/pallas_call | solution.py:674
  78.1 2.3 %emit.1 = (f32[32,2,2,4,256]{4,3,2,1,0:T(4,128)}, f32[16,128,128]{2,1,0:T(8,128)}) custom-call(f32[32,2,2,4,256]{4,3,2,1,0:T(4,128)} %get-tuple-element.6.revised_in, f32[16,128,128]{2,1,0:T(8,128)} %get-tuple-element.7.pair_in), custom_call_target="tpu_custom_call" | custom-call | tf_op jit(solution)/shard_map/emit/pallas_call | solution.py:752

commit v6 on v5

--- a/solution.py
+++ b/solution.py
@@ -152,18 +152,23 @@
     def spread(p):
         for i in (1, 3, 2):
             send(unit(p, 0, 0), unit(p, 0, 0), bias_send, bias_recv.at[1 + 10 * p], first_axis(p, i))
+        for k, sign in steps:
+            send(unit(p, 0, 0), unit(p, 0, 0), bias_send, bias_recv.at[3 + 10 * p + k], second_axis(p, sign))
 
     def spread_line(p):
         drain(bias_all.at[0, 0, 0:3], bias_recv.at[1 + 10 * p])
-        for k, sign in steps:
-            send(line(p, 0, k), line(p, 0, k), bias_send, bias_recv.at[5 + 10 * p + k], second_axis(p, sign))
-        for k, sign in steps:
-            send(line(p, 0, 1 - k), line(p, 0, 1 - k), bias_send,
-                 bias_recv.at[7 + 10 * p + k], second_axis(p, sign))
+        for base, other in ((5, 0), (7, 1)):
+            for i in (1, 3, 2):
+                for k, sign in steps:
+                    piece = unit(p, i, 0, (k + other) % 2)
+                    send(piece, piece, bias_send, bias_recv.at[base + 10 * p + k], second_axis(p, sign))
+
+    three = bias_all.at[0, 0, 0:3, 0]
 
     def forward_line(p):
         for k, sign in steps:
-            drain(line(0, 0, 0), bias_recv.at[5 + 10 * p + k])
+            drain(bias_ref, bias_recv.at[3 + 10 * p + k])
+            drain(three, bias_recv.at[5 + 10 * p + k])
             send(line(p, -sign, k), line(p, -sign, k), bias_send,
                  bias_recv.at[9 + 10 * p + k], second_axis(p, sign))
 
@@ -238,6 +243,7 @@
             pieces += [piece, gap] if s2 == 0 else [gap, piece]
         join_h[s2], join_l[s2] = split(jnp.concatenate(pieces, axis=0))
 
+    own_path(forward_line)
     for i, (src, dst) in enumerate(late):
         pltpu.make_async_copy(src, dst, fetch.at[i]).wait()
 
@@ -294,15 +300,14 @@
 
         @pl.when(step == 1)
         def _():
-            own_path(forward_line)
             other_path(forward_line)
             for p in range(2):
-                drain(line(0, 0, 0), bias_recv.at[7 + 10 * p + 1])
+                drain(three, bias_recv.at[7 + 10 * p + 1])
 
         @pl.when(step == 2)
         def _():
             for p in range(2):
-                drain(line(0, 0, 0), bias_recv.at[7 + 10 * p])
+                drain(three, bias_recv.at[7 + 10 * p])
 
         @pl.when(step == 3)
         def _():

time: 80.7 us -> 79.9 us (0.990); the launches traced: 80.5 us -> 78.6 us
  Pallas kernels: 79.7 us -> 77.8 us
    pallas_call x1, Pallas kernels: 77.5 us -> 75.6 us  [body(): pl.pallas_call(kernel, out_shape=[jax.ShapeDtypeStruct((32, 2, 2, 4, 256)...]
where the time goes in v6:
time: 79.9 us; the launch traced here: 78.6 us
  Pallas kernels  77.8 us (97%)
  between operations  0.8 us (1%)
    pallas_call x1, Pallas kernels, body(): pl.pallas_call(kernel, out_shape=[jax.ShapeDtypeStruct((32, 2, 2, 4, 256)...  75.6 us
    pallas_call x1, Pallas kernels, body(): pl.pallas_call(emit_kernel, out_shape=[jax.ShapeDtypeStruct((32, 2, 2, 4,...  2.26 us

profile of v6, /device:TPU:1, one launch (start us, length us, event | category | flops | bytes accessed | tf_op | source)
XLA Modules:
  0.0 78.6 jit_solution(5009296184874023303)
XLA Ops:
  0.6 75.6 %msa_block.1 = (f32[32,2,2,4,256]{4,3,2,1,0:T(4,128)}, f32[16,128,128]{2,1,0:T(8,128)}) custom-call(f32[4,32,2,8,256]{4,3,2,1,0:T(8,128)} %bitcast.6, f32[2,16,512]{2,1,0:T(8,128)} %bias_ref.1, s32[1,512]{1,0:T(1,128)} %bitcast.9, f32[2]{0:T(128)} %offset_ref.1, f32[4,64,256]{2,1,0:T(8,128)} %bitcast.7, f32[64,256]{1,0:T(8,128)} %final_in_ref.1, ...), custom_call_target="tpu_custom_call" | custom-call | tf_op jit(solution)/shard_map/msa_block/pallas_call | solution.py:679
  76.2 2.3 %emit.1 = (f32[32,2,2,4,256]{4,3,2,1,0:T(4,128)}, f32[16,128,128]{2,1,0:T(8,128)}) custom-call(f32[32,2,2,4,256]{4,3,2,1,0:T(4,128)} %get-tuple-element.6.revised_in, f32[16,128,128]{2,1,0:T(8,128)} %get-tuple-element.7.pair_in), custom_call_target="tpu_custom_call" | custom-call | tf_op jit(solution)/shard_map/emit/pallas_call | solution.py:757

commit v7 on v6

--- a/solution.py
+++ b/solution.py
@@ -293,7 +293,7 @@
 
             return carry
 
-        lax.fori_loop(0, 8, send_x, 0)
+        lax.fori_loop(0, 8, send_x, 0, unroll=True)
 
     def attend(step, carry):
         x_now, z_now = turned(step)

time: 79.9 us -> 79.6 us (level)
  no operation moved by 1% of the time
where the time goes in v7:
time: 79.6 us; the launch traced here: 78.8 us
  Pallas kernels  77.9 us (98%)
  between operations  0.8 us (1%)
    pallas_call x1, Pallas kernels, body(): pl.pallas_call(kernel, out_shape=[jax.ShapeDtypeStruct((32, 2, 2, 4, 256)...  75.7 us
    pallas_call x1, Pallas kernels, body(): pl.pallas_call(emit_kernel, out_shape=[jax.ShapeDtypeStruct((32, 2, 2, 4,...  2.26 us

profile of v7, /device:TPU:1, one launch (start us, length us, event | category | flops | bytes accessed | tf_op | source)
XLA Modules:
  0.0 78.8 jit_solution(6647420673545395440)
XLA Ops:
  0.6 75.7 %msa_block.1 = (f32[32,2,2,4,256]{4,3,2,1,0:T(4,128)}, f32[16,128,128]{2,1,0:T(8,128)}) custom-call(f32[4,32,2,8,256]{4,3,2,1,0:T(8,128)} %bitcast.6, f32[2,16,512]{2,1,0:T(8,128)} %bias_ref.1, s32[1,512]{1,0:T(1,128)} %bitcast.9, f32[2]{0:T(128)} %offset_ref.1, f32[4,64,256]{2,1,0:T(8,128)} %bitcast.7, f32[64,256]{1,0:T(8,128)} %final_in_ref.1, ...), custom_call_target="tpu_custom_call" | custom-call | tf_op jit(solution)/shard_map/msa_block/pallas_call | solution.py:679
  76.3 2.3 %emit.1 = (f32[32,2,2,4,256]{4,3,2,1,0:T(4,128)}, f32[16,128,128]{2,1,0:T(8,128)}) custom-call(f32[32,2,2,4,256]{4,3,2,1,0:T(4,128)} %get-tuple-element.6.revised_in, f32[16,128,128]{2,1,0:T(8,128)} %get-tuple-element.7.pair_in), custom_call_target="tpu_custom_call" | custom-call | tf_op jit(solution)/shard_map/emit/pallas_call | solution.py:757
